TPU v7x, 32 devices: a whole 2x2x4 slice. The times are simulated.
32 devices in a mesh: district: 2 (over x), tiles: 16 (over z, y, core).
Axes of the slice: x: 2, y: 2, z: 4, core: 2. Of those that a mesh axis runs over, the one named last changes fastest.
Arguments:
- sky: bfloat16 [336, 2306], P('district'), parts along dimension 0, may hold values from -6 to 6
- coeffs: bfloat16 [2306, 32768], P(None, ('district', 'tiles')), parts along dimension 1, may hold values from -0.125 to 0.125
- albedo: float32 [32768], P(('district', 'tiles')), parts along dimension 0, may hold values from 0.1 to 0.9
- view_blocks: bfloat16 [2048, 128, 128], P(('district', 'tiles')), parts along dimension 0, may hold values from -0.1875 to 0.1875
- block_rows: int32 [2048], P(('district', 'tiles')), parts along dimension 0, may hold values from 0 to 127, as said below
- block_cols: int32 [2048], P(('district', 'tiles')), parts along dimension 0, may hold values from 0 to 127, as said below
- counts: int32 [32], P(('district', 'tiles')), parts along dimension 0, may hold values from 8 to 64, as said below
Outputs:
- irradiance: float32 [168, 32768], P(None, ('district', 'tiles')), parts along dimension 1
There are 2 independent parts, one for each index of `district`. A program takes and returns all parts, laid end to end along the dimension named above; each array names one. Nothing has to cross between parts.
Inputs may be any that keep to these rules, and one draw needn't show every extreme that they name: `block_rows`: slots of group g (slots g * 64 to (g + 1) * 64 - 1) name receiving blocks of group g's own tiles, that is g * 8 to (g + 1) * 8 - 1. `block_cols`: the slots of one group name at most 2 distinct sending blocks among the tiles of any one group, and exactly 2 among those of some group. Slots of group g at positions counts[g] and beyond are unused; some group has all 64 slots live.
All inputs are finite; a program needn't handle non-finite values.
Results may differ from a plain program's by a relative error of at most 0.0011.
Values may be sent and summed in bfloat16 or wider, within the bound.
No kernel may reach another device: no remote copies, remote signals or barrier semaphores. Data moves between devices by JAX's collectives and lax.ppermute only.
A program may use at most 128 MiB of HBM per device.

v0:
```python
import jax
import jax.numpy as jnp
from jax import lax
from jax.sharding import PartitionSpec as P


def per_device(sky, coeffs, albedo, view_blocks, block_rows, block_cols, counts):
    direct = jnp.dot(sky, coeffs, preferred_element_type=jnp.float32)
    emitted = (albedo[None, :] * direct).astype(jnp.bfloat16)
    hour_count, tile_count = direct.shape
    block_size = view_blocks.shape[1]
    slot_count = view_blocks.shape[0]
    per_group = tile_count // block_size
    peers = lax.axis_size("tiles")
    my_index = lax.axis_index("tiles")
    everything = lax.all_gather(emitted, "tiles", axis=1, tiled=True)
    source_pool = everything.reshape(hour_count, peers * per_group, block_size)
    sources = jnp.take(source_pool, block_cols, axis=1)
    contrib = jnp.einsum("bij,hbj->bhi", view_blocks, sources, preferred_element_type=jnp.float32)
    live_slots = jnp.arange(slot_count, dtype=jnp.int32) < counts[0]
    local_rows = block_rows - my_index * per_group
    onehot = (local_rows[None, :] == jnp.arange(per_group, dtype=jnp.int32)[:, None]) & live_slots[
        None, :
    ]
    reflected = jnp.einsum(
        "rb,bhi->hri", onehot.astype(jnp.float32), contrib, precision=lax.Precision.HIGHEST
    )
    return direct + reflected.reshape(hour_count, tile_count)


def solution(mesh):
    in_specs = (
        P("district", None),
        P(None, ("district", "tiles")),
        P(("district", "tiles")),
        P(("district", "tiles"), None, None),
        P(("district", "tiles")),
        P(("district", "tiles")),
        P(("district", "tiles")),
    )
    out_specs = P(None, ("district", "tiles"))
    return jax.shard_map(
        per_device, mesh=mesh, in_specs=in_specs, out_specs=out_specs, check_vma=False
    )
```

profile of v0, /device:TPU:0, one launch (start us, length us, event | category | flops | bytes accessed | tf_op | source)
XLA Modules:
  0.0 96.0 jit_solution(9224806658957747345)
XLA Ops:
  6.5 0.0 copy-start
  6.5 0.0 copy-start.1
  6.5 0.0 copy-start.2
  6.5 0.0 all-gather.2.cloned.1.call-start
  6.5 4.6 %multiply_convert_fusion = (bf16[168,1024]{1,0:T(8,128)(2,1)}, f32[168,1024]{1,0:T(8,128)S(1)}) fusion(f32[1024]{0:T(1024)} %param.9, bf16[168,2306]{1,0:T(8,128)(2,1)} %param.7, bf16[2306,1024]{1,0:T(8,128)(2,1)} %param.8), kind=kOutput, calls=%fused_computation.10 | convolution fusion | flops 793755648 | bytes 6533792 | tf_op jit(solution)/shard_map/dot_general | solution.py:8
  11.1 0.0 all-gather.2.cloned.1.call-update
  11.8 0.0 copy-done.1
  11.9 0.0 copy-done.2
  11.9 59.5 %all-gather.2.cloned.1.call-done = bf16[168,16384]{1,0:T(8,128)(2,1)} async-done(((bf16[168,1024]{1,0:T(8,128)(2,1)}), bf16[168,16384]{1,0:T(8,128)(2,1)}) %all-gather.2.cloned.1.call-update) | async-done | bytes 5505040 | tf_op jit(solution)/shard_map/all_gather | solution.py:16
  71.4 6.0 %copy_bitcast_fusion = bf16[168,128,128]{2,0,1:T(8,128)(2,1)} fusion(bf16[168,16384]{1,0:T(8,128)(2,1)} %all-gather.2.cloned.1.call-done), kind=kLoop, calls=%fused_computation.1 | loop fusion | bytes 11010048 | tf_op jit(solution)/shard_map/reshape | solution.py:17
  77.4 5.0 %gather_fusion = bf16[64,168,128]{2,1,0:T(8,128)(2,1)} fusion(bf16[168,128,128]{2,0,1:T(8,128)(2,1)} %copy_bitcast_fusion, s32[1024]{0:T(1024)S(1)} %pad_clamp_fusion), kind=kCustom, calls=%fused_computation | custom fusion | bytes 5505280 | tf_op jit(solution)/shard_map/jit(_take)/gather | solution.py:18
  82.4 0.0 copy-done
  82.4 3.4 %fusion.2 = f32[64,168,128]{2,1,0:T(8,128)S(1)} fusion(bf16[64,128,128]{2,1,0:T(8,128)(2,1)S(1)} %copy-done, bf16[64,168,128]{2,1,0:T(8,128)(2,1)} %gather_fusion, pred[64]{0:T(512)(128)(4,1)S(1)} %compare_and_fusion), kind=kOutput, calls=%fused_computation.4 | convolution fusion | flops 353697792 | bytes 10354752 | tf_op jit(solution)/shard_map/bij,hbj->bhi/dot_general | solution.py:19
  85.8 2.3 %fusion = f32[168,128,8]{1,2,0:T(8,128)S(1)} fusion(f32[64,168,128]{2,1,0:T(8,128)S(1)} %fusion.2, s32[64]{0:T(128)S(1)} %broadcast_subtract_fusion, pred[64]{0:T(512)(128)(4,1)S(1)} %iota_compare_fusion.1), kind=kOutput, calls=%fused_computation.2 | convolution fusion | flops 132121600 | bytes 6193472 | tf_op jit(solution)/shard_map/rb,bhi->hri/dot_general | solution.py:25
  88.1 1.0 %bitcast_add_fusion = f32[168,1024]{1,0:T(8,128)} fusion(f32[168,1024]{1,0:T(8,128)S(1)} %get-tuple-element.6, f32[21,8,8,128]{3,2,1,0:T(8,128)S(1)} %bitcast.20), kind=kLoop, calls=%fused_computation.9 | loop fusion | flops 172032 | bytes 2064384 | tf_op jit(solution)/shard_map/add | solution.py:28
  (5 shorter events, 0.0 us)
Async XLA Ops:
  6.5 75.9 %copy-start = (bf16[64,128,128]{2,1,0:T(8,128)(2,1)S(1)}, bf16[64,128,128]{2,1,0:T(8,128)(2,1)}, u32[]{:S(2)}) copy-start(bf16[64,128,128]{2,1,0:T(8,128)(2,1)} %param.10) | copy-start | bytes 6291460
  6.5 5.3 %copy-start.1 = (s32[64]{0:T(128)S(1)}, s32[64]{0:T(128)}, u32[]{:S(2)}) copy-start(s32[64]{0:T(128)} %param.12) | copy-start | bytes 772
  6.5 5.3 %copy-start.2 = (s32[64]{0:T(128)S(1)}, s32[64]{0:T(128)}, u32[]{:S(2)}) copy-start(s32[64]{0:T(128)} %param.11) | copy-start | bytes 772
  6.5 64.9 %all-gather.2.cloned.1.call-start = ((), (), s32[]{:S(2)}) async-start(), calls=%async_computation | async-start | bytes 5849088 | tf_op jit(solution)/shard_map/all_gather | solution.py:16
Sparse Core Ops, SparseCore 0:
  11.3 60.1 all-gather.1
where the time goes:
time: 96.2 us; the launch traced here: 96 us
  waiting for transfers between devices  59.5 us (62%)
  between operations  14.1 us (15%)
  local copies, waits for them, and re-layouts  11 us (11%)
  matrix products  10.3 us (11%)
  other arithmetic  1.05 us (1%)
    all_gather x1, waiting for transfers between devices, per_device(): everything = lax.all_gather(emitted, 'tiles', axis=1, tiled=True)  59.5 us
    reshape x1, local copies, waits for them, and re-layouts, per_device(): source_pool = everything.reshape(hour_count, peers * per_group, block_size)  5.98 us
    gather x1, local copies, waits for them, and re-layouts, per_device(): sources = jnp.take(source_pool, block_cols, axis=1)  5.02 us
    dot_general x1, matrix products, per_device(): direct = jnp.dot(sky, coeffs, preferred_element_type=jnp.float32)  4.58 us
    dot_general x1, matrix products, per_device(): jnp.einsum('bij,hbj->bhi', view_blocks, sources, preferred_element_type=j...  3.42 us
    dot_general x1, matrix products, per_device(): jnp.einsum('rb,bhi->hri', onehot.astype(jnp.float32), contrib, precision=...  2.27 us
  transfers between devices with their start and end apart: 1, of which 1 were waited for; matrix products, arithmetic and copies ran while one was open for 0% of the time, Pallas kernels for 0%

commit v1 on v0

v1 whole, which is shorter than its diff:
```python
import functools

import jax
import jax.numpy as jnp
from jax import lax
from jax.experimental import pallas as pl
from jax.experimental.pallas import tpu as pltpu
from jax.sharding import PartitionSpec as P

NEAR = 8
AT_ONCE = 8
SMEM = pl.BlockSpec(memory_space=pltpu.SMEM)
VMEM = pl.BlockSpec(memory_space=pltpu.VMEM)
ANY = pl.BlockSpec(memory_space=pl.ANY)


def direct_kernel(sky_ref, coeffs_ref, albedo_ref, direct_ref, emitted_ref):
    direct = jnp.dot(sky_ref[...], coeffs_ref[...], preferred_element_type=jnp.float32)
    direct_ref[...] = direct
    emitted = (albedo_ref[...] * direct).astype(jnp.bfloat16)
    block = emitted_ref.shape[2]
    for at in range(emitted_ref.shape[0]):
        emitted_ref[at] = emitted[:, at * block : (at + 1) * block]


def direct_and_emitted(sky, coeffs, albedo, block, width):
    hours, patches = sky.shape
    tiles = coeffs.shape[1]
    return pl.pallas_call(
        direct_kernel,
        grid=(tiles // width,),
        in_specs=[
            pl.BlockSpec((hours, patches), lambda i: (0, 0)),
            pl.BlockSpec((patches, width), lambda i: (0, i)),
            pl.BlockSpec((1, width), lambda i: (0, i)),
        ],
        out_specs=[
            pl.BlockSpec((hours, width), lambda i: (0, i)),
            pl.BlockSpec((width // block, hours, block), lambda i: (i, 0, 0)),
        ],
        out_shape=[
            jax.ShapeDtypeStruct((hours, tiles), jnp.float32),
            jax.ShapeDtypeStruct((tiles // block, hours, block), jnp.bfloat16),
        ],
        compiler_params=pltpu.CompilerParams(vmem_limit_bytes=56 * 2**20),
        name="direct",
    )(sky, coeffs, albedo)


def pack_kernel(wanted, me_ref, table_ref, *refs):
    count = len(wanted)
    held, outs, sems = refs[: -count - 1], refs[-count - 1 : -1], refs[-1]
    copies = []
    for out, sends in zip(outs, wanted):
        for at, (which, bits, row, end) in enumerate(sends):
            block = table_ref[row, 2 * (me_ref[0] ^ bits) + end]
            copies.append(pltpu.make_async_copy(held[which].at[block], out.at[at], sems.at[len(copies)]))
    for copy in copies:
        copy.start()
    for copy in copies:
        copy.wait()


def pack(me, table, held, wanted):
    return pl.pallas_call(
        functools.partial(pack_kernel, wanted),
        in_specs=[SMEM, SMEM] + [VMEM] * len(held),
        out_specs=[ANY] * len(wanted),
        out_shape=[jax.ShapeDtypeStruct((len(sends),) + held[0].shape[1:], held[0].dtype) for sends in wanted],
        scratch_shapes=[pltpu.SemaphoreType.DMA((sum(map(len, wanted)),))],
        compiler_params=pltpu.CompilerParams(vmem_limit_bytes=24 * 2**20),
        name="pack",
    )(me, table, *held)


def plan_kernel(blocks, rooms, me_ref, count_ref, rows_ref, cols_ref, hi_ref, phase_ref, base_ref, order_ref, size_ref):
    phases, places = order_ref.shape
    for at in range(phases):
        size_ref[at] = 0

    def clear(i, carry):
        for at in range(phases):
            order_ref[at, i] = rooms[at] * 4096
        return carry

    lax.fori_loop(0, places, clear, 0)

    def step(slot, carry):
        col = cols_ref[slot]
        group = col // blocks
        kind = group ^ me_ref[0]
        inside = col - group * blocks
        local = (kind & (NEAR - 2)) == 0
        end = (inside == hi_ref[group]).astype(jnp.int32)
        source = base_ref[kind] + jnp.where(local, inside, end)
        row = rows_ref[slot] - me_ref[0] * blocks
        phase = phase_ref[kind]
        at = size_ref[phase]
        order_ref[phase, at] = slot + row * 256 + source * 4096
        size_ref[phase] = at + 1
        return carry

    lax.fori_loop(0, count_ref[0], step, 0)


def plan(me, counts, rows, cols, hi, phase, base, blocks, rooms):
    return pl.pallas_call(
        functools.partial(plan_kernel, blocks, rooms),
        in_specs=[SMEM] * 7,
        out_specs=[SMEM, SMEM],
        out_shape=[
            jax.ShapeDtypeStruct((len(rooms), rows.shape[0] + AT_ONCE), jnp.int32),
            jax.ShapeDtypeStruct((len(rooms),), jnp.int32),
        ],
        name="plan",
    )(me, counts, rows, cols, hi, phase, base)


def reflect_kernel(phase, order_ref, size_ref, total_ref, views_ref, *refs):
    sources, out_ref, pool, sems = refs[:-3], refs[-3], refs[-2], refs[-1]
    copies = []
    room = 0
    for number, source in enumerate(sources):
        length = source.shape[0]
        copies.append(pltpu.make_async_copy(source, pool.at[pl.ds(room, length)], sems.at[number]))
        room += length
    for copy in copies:
        copy.start()
    out_ref[...] = total_ref[...]
    pool[room] = jnp.zeros(pool.shape[1:], pool.dtype)
    for copy in copies:
        copy.wait()
    block = views_ref.shape[1]

    def step(i, carry):
        entries = [order_ref[phase, i * AT_ONCE + k] for k in range(AT_ONCE)]
        parts = [
            lax.dot_general(
                pool[entry // 4096],
                views_ref[entry & 255],
                (((1,), (1,)), ((), ())),
                preferred_element_type=jnp.float32,
            )
            for entry in entries
        ]
        for entry, part in zip(entries, parts):
            columns = pl.ds(pl.multiple_of(((entry // 256) & 15) * block, block), block)
            out_ref[:, columns] += part
        return carry

    lax.fori_loop(0, (size_ref[phase] + AT_ONCE - 1) // AT_ONCE, step, 0)


def reflect(phase, order, size, total, views, sources):
    room = sum(source.shape[0] for source in sources)
    return pl.pallas_call(
        functools.partial(reflect_kernel, phase),
        in_specs=[SMEM, SMEM, VMEM, VMEM] + [ANY] * len(sources),
        out_specs=VMEM,
        out_shape=jax.ShapeDtypeStruct(total.shape, total.dtype),
        scratch_shapes=[
            pltpu.VMEM((room + 1,) + sources[0].shape[1:], sources[0].dtype),
            pltpu.SemaphoreType.DMA((len(sources),)),
        ],
        compiler_params=pltpu.CompilerParams(vmem_limit_bytes=24 * 2**20),
        name="reflect",
    )(order, size, total, views, *sources)


def per_device(sky, coeffs, albedo, view_blocks, block_rows, block_cols, counts):
    peers = lax.axis_size("tiles")
    me = lax.axis_index("tiles").astype(jnp.int32).reshape(1)
    slots, block = view_blocks.shape[:2]
    blocks = coeffs.shape[1] // block
    rest = peers // NEAR - 1
    far = [NEAR * k for k in range(1, rest + 1)]
    steps = range(2, NEAR, 2)

    def swap(x, bits):
        return lax.ppermute(x, "tiles", [(i, i ^ bits) for i in range(peers)])

    direct, emitted = direct_and_emitted(sky, coeffs, albedo.reshape(1, -1), block, 2 * block)
    block_cols, counts, emitted = lax.optimization_barrier((block_cols, counts, emitted))

    far_held = [swap(emitted, bits) for bits in far]
    near_held = [emitted, swap(emitted, 1)]

    live = jnp.arange(slots, dtype=jnp.int32) < counts[0]
    reads = (block_cols // blocks == jnp.arange(peers, dtype=jnp.int32)[:, None]) & live
    inside = block_cols % blocks
    lo = jnp.min(jnp.where(reads, inside, blocks - 1), axis=1)
    hi = jnp.max(jnp.where(reads, inside, 0), axis=1)
    table = jnp.stack([lo, hi], axis=1).reshape(1, 2 * peers)
    step = 2
    while step < NEAR:
        table = jnp.concatenate([table, swap(table, step)])
        step *= 2

    phase_of, base_of = [], []
    for kind in range(peers):
        core, row, h = kind % 2, kind % NEAR // 2, kind // NEAR - 1
        if h < 0:
            phase_of.append(0)
            base_of.append(blocks * core if row == 0 else 2 * blocks + 4 * (row - 1) + 2 * core)
        elif row == 0:
            phase_of.append(1)
            base_of.append(blocks * (2 * h + core))
        elif row == 1:
            phase_of.append(1)
            base_of.append(2 * blocks * rest + 4 * h + 2 * core)
        else:
            phase_of.append(2)
            base_of.append(4 * rest * (row - 2) + 4 * h + 2 * core)
    rooms = [2 * blocks + 4 * len(steps), (2 * blocks + 4) * rest, 4 * rest * (len(steps) - 1)]
    own = pack(me, table, near_held, [[(c, c, d // 2, end) for c in range(2) for end in range(2)] for d in steps])
    early = [swap(x, d) for x, d in zip(own, steps)]
    block_rows, _ = lax.optimization_barrier((block_rows, own[0]))
    order, size = plan(
        me,
        counts,
        block_rows,
        block_cols,
        hi,
        jnp.array(phase_of, jnp.int32),
        jnp.array(base_of, jnp.int32),
        blocks,
        rooms,
    )

    order, size, *far_held = lax.optimization_barrier((order, size, *far_held))

    held = [x for shard in far_held for x in (shard, swap(shard, 1))]
    others = pack(
        me,
        table,
        held,
        [
            [(2 * h + c, far[h] ^ c, d // 2, end) for h in range(rest) for c in range(2) for end in range(2)]
            for d in steps
        ],
    )
    late = {d: swap(x, d) for x, d in reversed(list(zip(others, steps)))}
    direct, _ = lax.optimization_barrier((direct, others[0]))
    total = reflect(0, order, size, direct, view_blocks, near_held + early)
    total = reflect(1, order, size, total, view_blocks, held + [late[2]])
    return reflect(2, order, size, total, view_blocks, [late[d] for d in steps[1:]])


def solution(mesh):
    in_specs = (
        P("district", None),
        P(None, ("district", "tiles")),
        P(("district", "tiles")),
        P(("district", "tiles"), None, None),
        P(("district", "tiles")),
        P(("district", "tiles")),
        P(("district", "tiles")),
    )
    out_specs = P(None, ("district", "tiles"))
    return jax.shard_map(
        per_device, mesh=mesh, in_specs=in_specs, out_specs=out_specs, check_vma=False
    )
```

time: 96.2 us -> 50.1 us (0.52)
  waiting for transfers between devices: 59.5 us -> 12.6 us
  Pallas kernels: 0 us -> 16.3 us
  starting transfers between devices: 0.01 us -> 14.7 us
  between operations: 14.1 us -> 0.79 us
  matrix products: 10.3 us -> 0 us
  local copies, waits for them, and re-layouts: 11 us -> 4.53 us
    all_gather x1 -> x0, waiting for transfers between devices: 59.5 us -> none  [per_device(): everything = lax.all_gather(emitted, 'tiles', axis=1, tiled=True)]
    pallas_call x0 -> x7, Pallas kernels: none -> 16.3 us  [the longest x3 5.81 us: reflect(): pl.pallas_call(functools.partial(reflect_kernel, phase), in_specs=[SMEM,...]
    ppermute x0 -> x11, starting transfers between devices: none -> 14.7 us  [swap(): return lax.ppermute(x, 'tiles', [(i, i ^ bits) for i in range(peers)])]
    ppermute x0 -> x11, waiting for transfers between devices: none -> 12.6 us  [swap(): return lax.ppermute(x, 'tiles', [(i, i ^ bits) for i in range(peers)])]
    dot_general x3 -> x0, matrix products: 10.3 us -> none  [the longest x1 4.58 us: per_device(): direct = jnp.dot(sky, coeffs, preferred_element_type=jnp.float32)]
    reshape x1, local copies, waits for them, and re-layouts: 5.98 us -> 0.09 us  [per_device(): table = jnp.stack([lo, hi], axis=1).reshape(1, 2 * peers)]
    gather x1 -> x0, local copies, waits for them, and re-layouts: 5.02 us -> none  [per_device(): sources = jnp.take(source_pool, block_cols, axis=1)]
    unnamed x6 -> x16, local copies, waits for them, and re-layouts: 0.01 us -> 4.36 us
  transfers between devices with their start and end apart: 1 -> 11, of which waited for: 1 -> 6; matrix products, arithmetic and copies ran while one was open for 0% -> 1% of each run, Pallas kernels for 0% -> 18%
where the time goes in v1:
time: 50.1 us; the launch traced here: 49.1 us
  Pallas kernels  16.3 us (33%)
  starting transfers between devices  14.7 us (29%)
  waiting for transfers between devices  12.6 us (25%)
  local copies, waits for them, and re-layouts  4.53 us (9%)
  between operations  0.79 us (2%)
    ppermute x11, starting transfers between devices, swap(): return lax.ppermute(x, 'tiles', [(i, i ^ bits) for i in range(peers)])  14.7 us
    ppermute x11, waiting for transfers between devices, swap(): return lax.ppermute(x, 'tiles', [(i, i ^ bits) for i in range(peers)])  12.6 us
    pallas_call x3, Pallas kernels, reflect(): pl.pallas_call(functools.partial(reflect_kernel, phase), in_specs=[SMEM,...  5.81 us
    pallas_call x1, Pallas kernels, direct_and_emitted(): pl.pallas_call(direct_kernel, grid=(tiles // width,), in_specs=[pl.BlockS...  5.24 us
    unnamed x16, local copies, waits for them, and re-layouts  4.36 us
    pallas_call x2, Pallas kernels, pack(): pl.pallas_call(functools.partial(pack_kernel, wanted), in_specs=[SMEM, SM...  2.98 us
    pallas_call x1, Pallas kernels, plan(): pl.pallas_call(functools.partial(plan_kernel, blocks, rooms), in_specs=[S...  2.26 us
  transfers between devices with their start and end apart: 11, of which 6 were waited for; matrix products, arithmetic and copies ran while one was open for 1% of the time, Pallas kernels for 18%

profile of v1, /device:TPU:0, one launch (start us, length us, event | category | flops | bytes accessed | tf_op | source)
XLA Modules:
  0.0 49.1 jit_solution(7853122737391221797)
XLA Ops:
  0.0 0.0 copy-start.7
  0.0 0.0 copy-start
  0.0 5.2 %direct.1 = (f32[168,1024]{1,0:T(8,128)}, bf16[8,168,128]{2,1,0:T(8,128)(2,1)}) custom-call(bf16[168,2306]{1,0:T(8,128)(2,1)} %sky_ref.1, bf16[2306,1024]{1,0:T(8,128)(2,1)} %coeffs_ref.1, f32[1,1024]{1,0:T(1,128)} %bitcast.7), custom_call_target="tpu_custom_call" | custom-call | tf_op jit(solution)/shard_map/direct/pallas_call | solution.py:29
  5.2 4.0 %collective-permute-start.3 = (bf16[8,168,128]{2,1,0:T(8,128)(2,1)}, bf16[8,168,128]{2,1,0:T(8,128)(2,1)S(1)}, u32[]{:S(2)}, u32[]{:S(2)}) collective-permute-start(bf16[8,168,128]{2,1,0:T(8,128)(2,1)} %get-tuple-element.26.refs_0_), channel_id=1, source_target_pairs={{0,8},{1,9},{2,10},{3,11},{4,12},{5,13},{6,14},{7,15},{8,0},{9,1},... | collective-permute-start | bytes 1032200 | tf_op jit(solution)/shard_map/ppermute | solution.py:180
  9.3 0.0 collective-permute-start.2
  9.9 0.0 copy-done.7
  10.0 0.1 select_reduce_fusion.1
  10.1 0.0 copy-start.6
  10.1 0.1 copy.12
  10.2 0.1 reshape.16
  10.3 1.6 %collective-permute-start = (s32[1,32]{1,0:T(1,128)S(1)}, s32[1,32]{1,0:T(1,128)S(1)}, u32[]{:S(2)}, u32[]{:S(2)}) collective-permute-start(s32[1,32]{1,0:T(1,128)S(1)} %reshape.16), channel_id=1, source_target_pairs={{0,2},{1,3},{2,0},{3,1},{4,6},{5,7},{6,4},{7,5},{8,10},{9,11},{10,... | collective-permute-start | bytes 392 | tf_op jit(solution)/shard_map/ppermute | solution.py:180
  11.9 2.0 %collective-permute-done = s32[1,32]{1,0:T(1,128)S(1)} collective-permute-done((s32[1,32]{1,0:T(1,128)S(1)}, s32[1,32]{1,0:T(1,128)S(1)}, u32[]{:S(2)}, u32[]{:S(2)}) %collective-permute-start) | collective-permute-done | bytes 160 | tf_op jit(solution)/shard_map/ppermute | solution.py:180
  13.9 1.6 %collective-permute-start.1 = (s32[2,32]{1,0:T(2,128)S(1)}, s32[2,32]{1,0:T(2,128)S(1)}, u32[]{:S(2)}, u32[]{:S(2)}) collective-permute-start(s32[2,32]{1,0:T(2,128)S(1)} %pad_add_fusion.2), channel_id=1, source_target_pairs={{0,4},{1,5},{2,6},{3,7},{4,0},{5,1},{6,2},{7,3},{8,12},{9,13},{10,... | collective-permute-start | bytes 776 | tf_op jit(solution)/shard_map/ppermute | solution.py:180
  15.5 2.0 %collective-permute-done.1 = s32[2,32]{1,0:T(2,128)S(1)} collective-permute-done((s32[2,32]{1,0:T(2,128)S(1)}, s32[2,32]{1,0:T(2,128)S(1)}, u32[]{:S(2)}, u32[]{:S(2)}) %collective-permute-start.1) | collective-permute-done | bytes 288 | tf_op jit(solution)/shard_map/ppermute | solution.py:180
  17.5 0.0 collective-permute-done.2.refs_1_
  17.6 0.0 copy-start.1
  17.6 1.0 %copy-done.1 = bf16[8,168,128]{2,1,0:T(8,128)(2,1)S(1)} copy-done((bf16[8,168,128]{2,1,0:T(8,128)(2,1)S(1)}, bf16[8,168,128]{2,1,0:T(8,128)(2,1)}, u32[]{:S(2)}) %copy-start.1) | copy-done | bytes 344088
  18.5 1.5 %pack.2 = (bf16[4,168,128]{2,1,0:T(8,128)(2,1)S(1)}, bf16[4,168,128]{2,1,0:T(8,128)(2,1)S(1)}, bf16[4,168,128]{2,1,0:T(8,128)(2,1)S(1)}) custom-call(s32[1]{0:T(128)} %bitcast.me_ref, s32[4,32]{1,0:T(4,128)S(1)} %pad_add_fusion.table_ref, bf16[8,168,128]{2,1,0:T(8,128)(2,1)S(1)} %copy-done.1, bf16[8,168,128]{2,1,0:T(8,128)(2,1)S(1)} %collective-permute-done.2.refs_1_), custom_call_target="tpu_custom_call" | custom-call | tf_op jit(solution)/shard_map/pack/pallas_call | solution.py:65
  20.0 0.0 copy-done.6
  20.0 2.3 %plan.1 = (s32[3,72]{1,0:T(4,128)}, s32[3]{0:T(128)}) custom-call(s32[1]{0:T(128)} %bitcast.me_ref, s32[1]{0:T(128)} %copy.13.count_ref, s32[64]{0:T(128)} %rows_ref, s32[64]{0:T(128)} %cols_ref, s32[16]{0:T(128)} %copy-done.6, s32[16]{0:T(128)} %constant.42.clone.phase_ref, s32[16]{0:T(128)} %constant.43.clone.base_ref), custom_call_target="tpu_custom_call" | custom-call | tf_op jit(solution)/shard_map/plan/pallas_call | solution.py:107
  22.3 2.6 %collective-permute-done.3.refs_0_ = bf16[8,168,128]{2,1,0:T(8,128)(2,1)S(1)} collective-permute-done((bf16[8,168,128]{2,1,0:T(8,128)(2,1)}, bf16[8,168,128]{2,1,0:T(8,128)(2,1)S(1)}, u32[]{:S(2)}, u32[]{:S(2)}) %collective-permute-start.3) | collective-permute-done | bytes 344096 | tf_op jit(solution)/shard_map/ppermute | solution.py:180
  24.9 0.0 collective-permute-start.4
  24.9 0.8 %collective-permute-start.6 = (bf16[4,168,128]{2,1,0:T(8,128)(2,1)S(1)}, bf16[4,168,128]{2,1,0:T(8,128)(2,1)S(1)}, u32[]{:S(2)}, u32[]{:S(2)}) collective-permute-start(bf16[4,168,128]{2,1,0:T(8,128)(2,1)S(1)} %get-tuple-element.37), channel_id=1, source_target_pairs={{0,4},{1,5},{2,6},{3,7},{4,0},{5,1},{6,2},{7,3},{8,12},{9,13},{10,... | collective-permute-start | bytes 516104 | tf_op jit(solution)/shard_map/ppermute | solution.py:180
  25.8 2.2 %collective-permute-start.7 = (bf16[4,168,128]{2,1,0:T(8,128)(2,1)S(1)}, bf16[4,168,128]{2,1,0:T(8,128)(2,1)S(1)}, u32[]{:S(2)}, u32[]{:S(2)}) collective-permute-start(bf16[4,168,128]{2,1,0:T(8,128)(2,1)S(1)} %get-tuple-element.38), channel_id=1, source_target_pairs={{0,6},{1,7},{2,4},{3,5},{4,2},{5,3},{6,0},{7,1},{8,14},{9,15},{10,... | collective-permute-start | bytes 516104 | tf_op jit(solution)/shard_map/ppermute | solution.py:180
  28.0 0.5 collective-permute-start.5
  28.4 0.0 collective-permute-done.4.refs_1_
  28.4 1.5 %pack.3 = (bf16[4,168,128]{2,1,0:T(8,128)(2,1)S(1)}, bf16[4,168,128]{2,1,0:T(8,128)(2,1)S(1)}, bf16[4,168,128]{2,1,0:T(8,128)(2,1)S(1)}) custom-call(s32[1]{0:T(128)} %bitcast.me_ref, s32[4,32]{1,0:T(4,128)S(1)} %pad_add_fusion.table_ref, bf16[8,168,128]{2,1,0:T(8,128)(2,1)S(1)} %collective-permute-done.3.refs_0_, ...), custom_call_target="tpu_custom_call" | custom-call | tf_op jit(solution)/shard_map/pack/pallas_call | solution.py:65
  29.9 0.9 %collective-permute-start.9 = (bf16[4,168,128]{2,1,0:T(8,128)(2,1)S(1)}, bf16[4,168,128]{2,1,0:T(8,128)(2,1)S(1)}, u32[]{:S(2)}, u32[]{:S(2)}) collective-permute-start(bf16[4,168,128]{2,1,0:T(8,128)(2,1)S(1)} %get-tuple-element.39), channel_id=1, source_target_pairs={{0,4},{1,5},{2,6},{3,7},{4,0},{5,1},{6,2},{7,3},{8,12},{9,13},{10,... | collective-permute-start | bytes 516104 | tf_op jit(solution)/shard_map/ppermute | solution.py:180
  30.8 1.5 %collective-permute-start.8 = (bf16[4,168,128]{2,1,0:T(8,128)(2,1)S(1)}, bf16[4,168,128]{2,1,0:T(8,128)(2,1)S(1)}, u32[]{:S(2)}, u32[]{:S(2)}) collective-permute-start(bf16[4,168,128]{2,1,0:T(8,128)(2,1)S(1)} %get-tuple-element.35), channel_id=1, source_target_pairs={{0,2},{1,3},{2,0},{3,1},{4,6},{5,7},{6,4},{7,5},{8,10},{9,11},{10,... | collective-permute-start | bytes 516104 | tf_op jit(solution)/shard_map/ppermute | solution.py:180
  32.4 0.0 collective-permute-done.6.refs_3_
  32.4 1.5 %collective-permute-start.10 = (bf16[4,168,128]{2,1,0:T(8,128)(2,1)S(1)}, bf16[4,168,128]{2,1,0:T(8,128)(2,1)S(1)}, u32[]{:S(2)}, u32[]{:S(2)}) collective-permute-start(bf16[4,168,128]{2,1,0:T(8,128)(2,1)S(1)} %get-tuple-element.40), channel_id=1, source_target_pairs={{0,6},{1,7},{2,4},{3,5},{4,2},{5,3},{6,0},{7,1},{8,14},{9,15},{10,... | collective-permute-start | bytes 516104 | tf_op jit(solution)/shard_map/ppermute | solution.py:180
  33.9 2.9 %collective-permute-done.7.refs_4_ = bf16[4,168,128]{2,1,0:T(8,128)(2,1)S(1)} collective-permute-done((bf16[4,168,128]{2,1,0:T(8,128)(2,1)S(1)}, bf16[4,168,128]{2,1,0:T(8,128)(2,1)S(1)}, u32[]{:S(2)}, u32[]{:S(2)}) %collective-permute-start.7) | collective-permute-done | bytes 172064 | tf_op jit(solution)/shard_map/ppermute | solution.py:180
  36.8 2.1 %collective-permute-done.5.refs_2_ = bf16[4,168,128]{2,1,0:T(8,128)(2,1)S(1)} collective-permute-done((bf16[4,168,128]{2,1,0:T(8,128)(2,1)S(1)}, bf16[4,168,128]{2,1,0:T(8,128)(2,1)S(1)}, u32[]{:S(2)}, u32[]{:S(2)}) %collective-permute-start.5) | collective-permute-done | bytes 172064 | tf_op jit(solution)/shard_map/ppermute | solution.py:180
  38.9 0.0 copy-done
  38.9 0.0 copy-start.2
  38.9 1.0 %copy-done.2 = bf16[8,168,128]{2,1,0:T(8,128)(2,1)S(1)} copy-done((bf16[8,168,128]{2,1,0:T(8,128)(2,1)S(1)}, bf16[8,168,128]{2,1,0:T(8,128)(2,1)}, u32[]{:S(2)}) %copy-start.2) | copy-done | bytes 344088
  39.9 0.0 copy-start.3
  39.9 1.1 %copy-done.3 = f32[168,1024]{1,0:T(8,128)S(1)} copy-done((f32[168,1024]{1,0:T(8,128)S(1)}, f32[168,1024]{1,0:T(8,128)}, u32[]{:S(2)}) %copy-start.3) | copy-done | bytes 688152
  41.0 0.0 copy-start.4
  41.0 0.7 %copy-done.4 = s32[3,72]{1,0:T(4,128)S(1)} copy-done((s32[3,72]{1,0:T(4,128)S(1)}, s32[3,72]{1,0:T(4,128)}, u32[]{:S(2)}) %copy-start.4) | copy-done | bytes 888
  41.7 0.0 copy-start.5
  41.7 0.6 %copy-done.5 = s32[3]{0:T(128)S(1)} copy-done((s32[3]{0:T(128)S(1)}, s32[3]{0:T(128)}, u32[]{:S(2)}) %copy-start.5) | copy-done | bytes 36
  42.3 2.0 %reflect.3.total_ref = f32[168,1024]{1,0:T(8,128)S(1)} custom-call(s32[3,72]{1,0:T(4,128)S(1)} %copy-done.4, s32[3]{0:T(128)S(1)} %copy-done.5, f32[168,1024]{1,0:T(8,128)S(1)} %copy-done.3, bf16[64,128,128]{2,1,0:T(8,128)(2,1)S(1)} %copy-done, bf16[8,168,128]{2,1,0:T(8,128)(2,1)S(1)} %copy-done.2, bf16[8,168,128]{2,1,0:T(8,128)(2,1)S(1)} %collective-permute-done.2.refs_1_, ...), custom_call_target="tpu_custom_call" | custom-call | tf_op jit(solution)/shard_map/reflect/pallas_call | solution.py:156
  44.3 1.0 %collective-permute-done.8.refs_2_ = bf16[4,168,128]{2,1,0:T(8,128)(2,1)S(1)} collective-permute-done((bf16[4,168,128]{2,1,0:T(8,128)(2,1)S(1)}, bf16[4,168,128]{2,1,0:T(8,128)(2,1)S(1)}, u32[]{:S(2)}, u32[]{:S(2)}) %collective-permute-start.8) | collective-permute-done | bytes 172064 | tf_op jit(solution)/shard_map/ppermute | solution.py:180
  45.3 1.5 %reflect.4.total_ref = f32[168,1024]{1,0:T(8,128)S(1)} custom-call(s32[3,72]{1,0:T(4,128)S(1)} %copy-done.4, s32[3]{0:T(128)S(1)} %copy-done.5, f32[168,1024]{1,0:T(8,128)S(1)} %reflect.3.total_ref, bf16[64,128,128]{2,1,0:T(8,128)(2,1)S(1)} %copy-done, bf16[8,168,128]{2,1,0:T(8,128)(2,1)S(1)} %collective-permute-done.3.refs_0_, ...), custom_call_target="tpu_custom_call" | custom-call | tf_op jit(solution)/shard_map/reflect/pallas_call | solution.py:156
  46.8 0.0 collective-permute-done.9.refs_0_
  46.8 0.0 collective-permute-done.10.refs_1_
  46.8 2.3 %reflect.5 = f32[168,1024]{1,0:T(8,128)} custom-call(s32[3,72]{1,0:T(4,128)S(1)} %copy-done.4, s32[3]{0:T(128)S(1)} %copy-done.5, f32[168,1024]{1,0:T(8,128)S(1)} %reflect.4.total_ref, bf16[64,128,128]{2,1,0:T(8,128)(2,1)S(1)} %copy-done, bf16[4,168,128]{2,1,0:T(8,128)(2,1)S(1)} %collective-permute-done.9.refs_0_, ...), custom_call_target="tpu_custom_call" | custom-call | tf_op jit(solution)/shard_map/reflect/pallas_call | solution.py:156
  (5 shorter events, 0.0 us)
Async XLA Ops:
  0.0 10.0 %copy-start.7 = (s32[64]{0:T(128)S(1)}, s32[64]{0:T(128)}, u32[]{:S(2)}) copy-start(s32[64]{0:T(128)} %cols_ref) | copy-start | bytes 772
  0.0 38.9 %copy-start = (bf16[64,128,128]{2,1,0:T(8,128)(2,1)S(1)}, bf16[64,128,128]{2,1,0:T(8,128)(2,1)}, u32[]{:S(2)}) copy-start(bf16[64,128,128]{2,1,0:T(8,128)(2,1)} %views_ref.5) | copy-start | bytes 6291460
  5.2 19.7 %collective-permute-start.3 = (bf16[8,168,128]{2,1,0:T(8,128)(2,1)}, bf16[8,168,128]{2,1,0:T(8,128)(2,1)S(1)}, u32[]{:S(2)}, u32[]{:S(2)}) collective-permute-start(bf16[8,168,128]{2,1,0:T(8,128)(2,1)} %get-tuple-element.26.refs_0_), channel_id=1, source_target_pairs={{0,8},{1,9},{2,10},{3,11},{4,12},{5,13},{6,14},{7,15},{8,0},{9,1},... | collective-permute-start | bytes 1032200 | tf_op jit(solution)/shard_map/ppermute | solution.py:180
  9.3 8.3 %collective-permute-start.2 = (bf16[8,168,128]{2,1,0:T(8,128)(2,1)}, bf16[8,168,128]{2,1,0:T(8,128)(2,1)S(1)}, u32[]{:S(2)}, u32[]{:S(2)}) collective-permute-start(bf16[8,168,128]{2,1,0:T(8,128)(2,1)} %get-tuple-element.26.refs_0_), channel_id=1, source_target_pairs={{0,1},{1,0},{2,3},{3,2},{4,5},{5,4},{6,7},{7,6},{8,9},{9,8},{10,11... | collective-permute-start | bytes 1032200 | tf_op jit(solution)/shard_map/ppermute | solution.py:180
  10.1 9.9 %copy-start.6 = (s32[16]{0:T(128)}, s32[16]{0:T(128)S(1)}, u32[]{:S(2)}) copy-start(s32[16]{0:T(128)S(1)} %get-tuple-element.42.hi_ref) | copy-start | bytes 196
  10.3 3.6 %collective-permute-start = (s32[1,32]{1,0:T(1,128)S(1)}, s32[1,32]{1,0:T(1,128)S(1)}, u32[]{:S(2)}, u32[]{:S(2)}) collective-permute-start(s32[1,32]{1,0:T(1,128)S(1)} %reshape.16), channel_id=1, source_target_pairs={{0,2},{1,3},{2,0},{3,1},{4,6},{5,7},{6,4},{7,5},{8,10},{9,11},{10,... | collective-permute-start | bytes 392 | tf_op jit(solution)/shard_map/ppermute | solution.py:180
  13.9 3.6 %collective-permute-start.1 = (s32[2,32]{1,0:T(2,128)S(1)}, s32[2,32]{1,0:T(2,128)S(1)}, u32[]{:S(2)}, u32[]{:S(2)}) collective-permute-start(s32[2,32]{1,0:T(2,128)S(1)} %pad_add_fusion.2), channel_id=1, source_target_pairs={{0,4},{1,5},{2,6},{3,7},{4,0},{5,1},{6,2},{7,3},{8,12},{9,13},{10,... | collective-permute-start | bytes 776 | tf_op jit(solution)/shard_map/ppermute | solution.py:180
  17.6 1.0 %copy-start.1 = (bf16[8,168,128]{2,1,0:T(8,128)(2,1)S(1)}, bf16[8,168,128]{2,1,0:T(8,128)(2,1)}, u32[]{:S(2)}) copy-start(bf16[8,168,128]{2,1,0:T(8,128)(2,1)} %get-tuple-element.26.refs_0_) | copy-start | bytes 1032196
  24.9 3.5 %collective-permute-start.4 = (bf16[8,168,128]{2,1,0:T(8,128)(2,1)S(1)}, bf16[8,168,128]{2,1,0:T(8,128)(2,1)S(1)}, u32[]{:S(2)}, u32[]{:S(2)}) collective-permute-start(bf16[8,168,128]{2,1,0:T(8,128)(2,1)S(1)} %collective-permute-done.3.refs_0_), channel_id=1, source_target_pairs={{0,1},{1,0},{2,3},{3,2},{4,5},{5,4},{6,7},{7,6},{8,9},{9,8},{10,11... | collective-permute-start | bytes 1032200 | tf_op jit(solution)/shard_map/ppermute | solution.py:180
  24.9 7.4 %collective-permute-start.6 = (bf16[4,168,128]{2,1,0:T(8,128)(2,1)S(1)}, bf16[4,168,128]{2,1,0:T(8,128)(2,1)S(1)}, u32[]{:S(2)}, u32[]{:S(2)}) collective-permute-start(bf16[4,168,128]{2,1,0:T(8,128)(2,1)S(1)} %get-tuple-element.37), channel_id=1, source_target_pairs={{0,4},{1,5},{2,6},{3,7},{4,0},{5,1},{6,2},{7,3},{8,12},{9,13},{10,... | collective-permute-start | bytes 516104 | tf_op jit(solution)/shard_map/ppermute | solution.py:180
  25.8 11.1 %collective-permute-start.7 = (bf16[4,168,128]{2,1,0:T(8,128)(2,1)S(1)}, bf16[4,168,128]{2,1,0:T(8,128)(2,1)S(1)}, u32[]{:S(2)}, u32[]{:S(2)}) collective-permute-start(bf16[4,168,128]{2,1,0:T(8,128)(2,1)S(1)} %get-tuple-element.38), channel_id=1, source_target_pairs={{0,6},{1,7},{2,4},{3,5},{4,2},{5,3},{6,0},{7,1},{8,14},{9,15},{10,... | collective-permute-start | bytes 516104 | tf_op jit(solution)/shard_map/ppermute | solution.py:180
  28.0 10.9 %collective-permute-start.5 = (bf16[4,168,128]{2,1,0:T(8,128)(2,1)S(1)}, bf16[4,168,128]{2,1,0:T(8,128)(2,1)S(1)}, u32[]{:S(2)}, u32[]{:S(2)}) collective-permute-start(bf16[4,168,128]{2,1,0:T(8,128)(2,1)S(1)} %get-tuple-element.27), channel_id=1, source_target_pairs={{0,2},{1,3},{2,0},{3,1},{4,6},{5,7},{6,4},{7,5},{8,10},{9,11},{10,... | collective-permute-start | bytes 516104 | tf_op jit(solution)/shard_map/ppermute | solution.py:180
  29.9 16.9 %collective-permute-start.9 = (bf16[4,168,128]{2,1,0:T(8,128)(2,1)S(1)}, bf16[4,168,128]{2,1,0:T(8,128)(2,1)S(1)}, u32[]{:S(2)}, u32[]{:S(2)}) collective-permute-start(bf16[4,168,128]{2,1,0:T(8,128)(2,1)S(1)} %get-tuple-element.39), channel_id=1, source_target_pairs={{0,4},{1,5},{2,6},{3,7},{4,0},{5,1},{6,2},{7,3},{8,12},{9,13},{10,... | collective-permute-start | bytes 516104 | tf_op jit(solution)/shard_map/ppermute | solution.py:180
  30.8 14.4 %collective-permute-start.8 = (bf16[4,168,128]{2,1,0:T(8,128)(2,1)S(1)}, bf16[4,168,128]{2,1,0:T(8,128)(2,1)S(1)}, u32[]{:S(2)}, u32[]{:S(2)}) collective-permute-start(bf16[4,168,128]{2,1,0:T(8,128)(2,1)S(1)} %get-tuple-element.35), channel_id=1, source_target_pairs={{0,2},{1,3},{2,0},{3,1},{4,6},{5,7},{6,4},{7,5},{8,10},{9,11},{10,... | collective-permute-start | bytes 516104 | tf_op jit(solution)/shard_map/ppermute | solution.py:180
  32.4 14.4 %collective-permute-start.10 = (bf16[4,168,128]{2,1,0:T(8,128)(2,1)S(1)}, bf16[4,168,128]{2,1,0:T(8,128)(2,1)S(1)}, u32[]{:S(2)}, u32[]{:S(2)}) collective-permute-start(bf16[4,168,128]{2,1,0:T(8,128)(2,1)S(1)} %get-tuple-element.40), channel_id=1, source_target_pairs={{0,6},{1,7},{2,4},{3,5},{4,2},{5,3},{6,0},{7,1},{8,14},{9,15},{10,... | collective-permute-start | bytes 516104 | tf_op jit(solution)/shard_map/ppermute | solution.py:180
  38.9 1.0 %copy-start.2 = (bf16[8,168,128]{2,1,0:T(8,128)(2,1)S(1)}, bf16[8,168,128]{2,1,0:T(8,128)(2,1)}, u32[]{:S(2)}) copy-start(bf16[8,168,128]{2,1,0:T(8,128)(2,1)} %get-tuple-element.26.refs_0_) | copy-start | bytes 1032196
  39.9 1.1 %copy-start.3 = (f32[168,1024]{1,0:T(8,128)S(1)}, f32[168,1024]{1,0:T(8,128)}, u32[]{:S(2)}) copy-start(f32[168,1024]{1,0:T(8,128)} %get-tuple-element.36.total_ref) | copy-start | bytes 2064388
  41.0 0.7 %copy-start.4 = (s32[3,72]{1,0:T(4,128)S(1)}, s32[3,72]{1,0:T(4,128)}, u32[]{:S(2)}) copy-start(s32[3,72]{1,0:T(4,128)} %get-tuple-element.31.order_ref) | copy-start | bytes 2596
  41.7 0.6 %copy-start.5 = (s32[3]{0:T(128)S(1)}, s32[3]{0:T(128)}, u32[]{:S(2)}) copy-start(s32[3]{0:T(128)} %get-tuple-element.32.size_ref) | copy-start | bytes 40

commit v2 on v0

v2 whole, which is shorter than its diff:
```python
import functools

import jax
import jax.numpy as jnp
from jax import lax
from jax.experimental import pallas as pl
from jax.experimental.pallas import tpu as pltpu
from jax.sharding import PartitionSpec as P

NEAR = 8
AT_ONCE = 8
SMEM = pl.BlockSpec(memory_space=pltpu.SMEM)
VMEM = pl.BlockSpec(memory_space=pltpu.VMEM)
ANY = pl.BlockSpec(memory_space=pl.ANY)
HBM = pl.BlockSpec(memory_space=pltpu.HBM)


def direct_kernel(width, sky_ref, coeffs_ref, albedo_ref, direct_ref, emitted_ref, sky, coeffs, direct, sems):
    blocks, _, block = emitted_ref.shape
    parts = coeffs.shape[0]
    whole_sky = pltpu.make_async_copy(sky_ref, sky, sems.at[2 * parts])
    copies = [
        pltpu.make_async_copy(coeffs_ref.at[:, pl.ds(at * width, width)], coeffs.at[at], sems.at[at])
        for at in range(parts)
    ]
    results = [
        pltpu.make_async_copy(direct.at[at], direct_ref.at[:, pl.ds(at * width, width)], sems.at[parts + at])
        for at in range(parts)
    ]
    copies[0].start()
    whole_sky.start()
    for copy in copies[1:]:
        copy.start()
    whole_sky.wait()
    for at in range(parts):
        copies[at].wait()
        part = jnp.dot(sky[...], coeffs[at], preferred_element_type=jnp.float32)
        direct[at] = part
        results[at].start()
        emitted = (albedo_ref[:, at * width : (at + 1) * width] * part).astype(jnp.bfloat16)
        for k in range(width // block):
            emitted_ref[at * (width // block) + k] = emitted[:, k * block : (k + 1) * block]
    for result in results:
        result.wait()


def direct_and_emitted(sky, coeffs, albedo, block, width):
    hours, patches = sky.shape
    tiles = coeffs.shape[1]
    parts = tiles // width
    return pl.pallas_call(
        functools.partial(direct_kernel, width),
        in_specs=[HBM, HBM, VMEM],
        out_specs=[HBM, VMEM],
        out_shape=[
            jax.ShapeDtypeStruct((hours, tiles), jnp.float32),
            pltpu.VMEM((tiles // block, hours, block), jnp.bfloat16),
        ],
        scratch_shapes=[
            pltpu.VMEM(sky.shape, sky.dtype),
            pltpu.VMEM((parts, patches, width), coeffs.dtype),
            pltpu.VMEM((parts, hours, width), jnp.float32),
            pltpu.SemaphoreType.DMA((2 * parts + 1,)),
        ],
        compiler_params=pltpu.CompilerParams(vmem_limit_bytes=60 * 2**20),
        name="direct",
    )(sky, coeffs, albedo)


def reads_kernel(blocks, groups, cols_ref, reads_ref):
    slots, width = cols_ref.shape[1], reads_ref.shape[1]
    group = lax.broadcasted_iota(jnp.int32, (groups, slots), 0)
    inside = jnp.broadcast_to(cols_ref[...], (groups, slots)) - group * blocks
    read = (inside >= 0) & (inside < blocks)
    lo = jnp.min(jnp.where(read, inside, blocks - 1), axis=1, keepdims=True)
    hi = jnp.max(jnp.where(read, inside, 0), axis=1, keepdims=True)
    group = lax.broadcasted_iota(jnp.int32, (groups, width), 0)
    lane = lax.broadcasted_iota(jnp.int32, (groups, width), 1)
    row = jnp.where(lane == group, lo, 0) + jnp.where(lane == group + groups, hi, 0)
    live = jnp.sum((cols_ref[...] >= 0).astype(jnp.int32), axis=1, keepdims=True)
    reads_ref[...] = jnp.sum(row, axis=0, keepdims=True) + jnp.where(lane[0:1] == 2 * groups, live, 0)


def blocks_read(cols, blocks, groups):
    width = -(-(2 * groups + 1) // 128) * 128
    return pl.pallas_call(
        functools.partial(reads_kernel, blocks, groups),
        in_specs=[VMEM],
        out_specs=VMEM,
        out_shape=jax.ShapeDtypeStruct((1, width), jnp.int32),
        compiler_params=pltpu.CompilerParams(vmem_limit_bytes=2**20),
        name="reads",
    )(cols.reshape(1, -1))


def pack_kernel(wanted, groups, me_ref, table_ref, *refs):
    held, outs = refs[: -len(wanted)], refs[-len(wanted) :]
    for out, (peer, sends) in zip(outs, wanted):
        for at, (which, bits, end) in enumerate(sends):
            out[at] = held[which][table_ref[peer, (me_ref[0] ^ bits) + groups * end]]


def pack(me, table, groups, held, wanted):
    return pl.pallas_call(
        functools.partial(pack_kernel, wanted, groups),
        in_specs=[SMEM, SMEM] + [VMEM] * len(held),
        out_specs=[VMEM] * len(wanted),
        out_shape=[pltpu.VMEM((len(sends),) + held[0].shape[1:], held[0].dtype) for _, sends in wanted],
        compiler_params=pltpu.CompilerParams(vmem_limit_bytes=24 * 2**20),
        name="pack",
    )(me, table, *held)


def plan_kernel(blocks, rooms, groups, me_ref, rows_ref, cols_ref, reads_ref, phase_ref, base_ref, local_ref, after_ref, order_ref):
    del after_ref
    phases, places = order_ref.shape

    def clear(i, carry):
        for at in range(phases):
            order_ref[at, i] = rooms[at] * 4096
        return carry

    lax.fori_loop(1, places, clear, 0)
    for at in range(phases):
        order_ref[at, 0] = 0

    def step(slot, carry):
        col = cols_ref[slot]
        group = col // blocks
        kind = group ^ me_ref[0]
        inside = col - group * blocks
        local = local_ref[kind] == 1
        end = (inside == reads_ref[0, groups + group]).astype(jnp.int32)
        source = base_ref[kind] + jnp.where(local, inside, end)
        row = rows_ref[slot] - me_ref[0] * blocks
        phase = phase_ref[kind]
        at = order_ref[phase, 0] + 1
        order_ref[phase, at] = slot + row * 256 + source * 4096
        order_ref[phase, 0] = at
        return carry

    lax.fori_loop(0, reads_ref[0, 2 * groups], step, 0)


def plan(me, rows, cols, reads, phase, base, local, after, blocks, rooms):
    return pl.pallas_call(
        functools.partial(plan_kernel, blocks, rooms, phase.shape[0]),
        in_specs=[SMEM] * 7 + [ANY],
        out_specs=SMEM,
        out_shape=jax.ShapeDtypeStruct((len(rooms), 1 + rows.shape[0] + AT_ONCE), jnp.int32),
        compiler_params=pltpu.CompilerParams(vmem_limit_bytes=2**20),
        name="plan",
    )(me, rows, cols, reads, phase, base, local, after)


def reflect_kernel(phase, order_ref, total_ref, views_ref, *refs):
    sources, (out_ref, pool, order, sems) = refs[:-4], refs[-4:]
    copies = [
        pltpu.make_async_copy(total_ref, out_ref, sems.at[len(sources)]),
        pltpu.make_async_copy(order_ref, order, sems.at[len(sources) + 1]),
    ]
    room = 0
    for number, source in enumerate(sources):
        length = source.shape[0]
        copies.append(pltpu.make_async_copy(source, pool.at[pl.ds(room, length)], sems.at[number]))
        room += length
    for copy in copies:
        copy.start()
    pool[room] = jnp.zeros(pool.shape[1:], pool.dtype)
    for copy in copies:
        copy.wait()
    block = views_ref.shape[1]

    def step(i, carry):
        entries = [order[phase, 1 + i * AT_ONCE + k] for k in range(AT_ONCE)]
        parts = [
            lax.dot_general(
                pool[entry // 4096],
                views_ref[entry & 255],
                (((1,), (1,)), ((), ())),
                preferred_element_type=jnp.float32,
            )
            for entry in entries
        ]
        for entry, part in zip(entries, parts):
            columns = pl.ds(pl.multiple_of(((entry // 256) & 15) * block, block), block)
            out_ref[:, columns] += part
        return carry

    lax.fori_loop(0, (order[phase, 0] + AT_ONCE - 1) // AT_ONCE, step, 0)


def reflect(phase, order, total, views, sources):
    room = sum(source.shape[0] for source in sources)
    return pl.pallas_call(
        functools.partial(reflect_kernel, phase),
        in_specs=[HBM, HBM if phase == 0 else ANY, VMEM] + [ANY] * len(sources),
        out_specs=VMEM,
        out_shape=jax.ShapeDtypeStruct(total.shape, total.dtype),
        scratch_shapes=[
            pltpu.VMEM((room + 1,) + sources[0].shape[1:], sources[0].dtype),
            pltpu.SMEM(order.shape, order.dtype),
            pltpu.SemaphoreType.DMA((len(sources) + 2,)),
        ],
        compiler_params=pltpu.CompilerParams(vmem_limit_bytes=24 * 2**20),
        name="reflect",
    )(order, total, views, *sources)


def per_device(sky, coeffs, albedo, view_blocks, block_rows, block_cols, counts):
    peers = lax.axis_size("tiles")
    me = lax.axis_index("tiles").astype(jnp.int32).reshape(1)
    block = view_blocks.shape[1]
    blocks = coeffs.shape[1] // block
    rest = peers // NEAR - 1
    far = [NEAR * k for k in range(1, rest + 1)]
    core, beside, below = 1, 2, 4

    def swap(x, bits):
        return lax.ppermute(x, "tiles", [(i, i ^ bits) for i in range(peers)])

    direct, emitted = direct_and_emitted(sky, coeffs, albedo.reshape(1, -1), block, 4 * block)
    counts, view_blocks, emitted = lax.optimization_barrier((counts, view_blocks, emitted))

    far_held = [swap(emitted, bits) for bits in far]
    below_held = swap(emitted, below)
    beside_held = swap(emitted, beside)

    live = jnp.arange(block_cols.shape[0], dtype=jnp.int32) < counts[0]
    reads = blocks_read(jnp.where(live, block_cols, -1), blocks, peers)
    core_reads = swap(reads, core)
    table = jnp.concatenate([reads, swap(reads, beside)])
    below_table = swap(table, below)

    (own,) = pack(
        me, core_reads, peers, [emitted, beside_held], [(0, [(h, h * beside, end) for h in range(2) for end in range(2)])]
    )
    own = swap(own, core)

    place = {
        0: (0, 0),
        beside: (0, blocks),
        core: (0, 2 * blocks),
        beside + core: (0, 2 * blocks + 2),
        below: (1, 2 * blocks * rest),
        below + core: (1, 2 * blocks * rest + blocks),
        below + beside + core: (1, 2 * blocks * (rest + 1) + 4 * rest),
        below + beside: (2, 4 * rest),
    }
    local = {0, beside, below, below + core}
    for h, bits in enumerate(far):
        for c in range(2):
            local.add(bits + c)
            place[bits + c] = (1, blocks * (2 * h + c))
            place[bits + beside + c] = (1, 2 * blocks * (rest + 1) + 4 * h + 2 * c)
            place[bits + below + c] = (2, 4 * h + 2 * c)
            place[bits + below + beside + c] = (2, 4 * rest + 2 + 4 * h + 2 * c)
    rooms = [2 * blocks + 4, 2 * blocks * (rest + 1) + 4 * rest + 2, 8 * rest + 2]
    order = plan(
        me,
        block_rows,
        block_cols,
        reads,
        jnp.array([place[kind][0] for kind in range(peers)], jnp.int32),
        jnp.array([place[kind][1] for kind in range(peers)], jnp.int32),
        jnp.array([int(kind in local) for kind in range(peers)], jnp.int32),
        own,
        blocks,
        rooms,
    )
    order, below_table, below_held, far_held = lax.optimization_barrier((order, below_table, below_held, far_held))
    table = jnp.concatenate([table, below_table])
    held = [x for shard in far_held for x in (shard, swap(shard, core))]
    below_pair = [below_held, swap(below_held, core)]

    wanted = [(2 * h + c, far[h] + c, end) for h in range(rest) for c in range(2) for end in range(2)]
    from_beside = [(2 * rest, below + core, end) for end in range(2)]
    from_below = [(2 * rest + 1, beside, end) for end in range(2)]
    sends = [(1, wanted + from_beside), (2, wanted + from_below), (3, wanted)]
    others = pack(me, table, peers, held + [below_pair[1], beside_held], sends)
    late = [swap(x, bits) for x, bits in zip(others, (beside, below, below + beside))]

    direct, _ = lax.optimization_barrier((direct, others[0]))
    total = reflect(0, order, direct, view_blocks, [emitted, beside_held, own])
    total = reflect(1, order, total, view_blocks, held + below_pair + late[:1])
    return reflect(2, order, total, view_blocks, late[1:])


def solution(mesh):
    in_specs = (
        P("district", None),
        P(None, ("district", "tiles")),
        P(("district", "tiles")),
        P(("district", "tiles"), None, None),
        P(("district", "tiles")),
        P(("district", "tiles")),
        P(("district", "tiles")),
    )
    out_specs = P(None, ("district", "tiles"))
    return jax.shard_map(
        per_device, mesh=mesh, in_specs=in_specs, out_specs=out_specs, check_vma=False
    )
```

time: 96.2 us -> 44.7 us (0.46)
  waiting for transfers between devices: 59.5 us -> 13.9 us
  starting transfers between devices: 0.01 us -> 15 us
  between operations: 14.1 us -> 0.79 us
  Pallas kernels: 0 us -> 13.3 us
  matrix products: 10.3 us -> 0 us
  local copies, waits for them, and re-layouts: 11 us -> 1.12 us
  other arithmetic: 1.05 us -> 0.02 us
    all_gather x1 -> x0, waiting for transfers between devices: 59.5 us -> none  [per_device(): everything = lax.all_gather(emitted, 'tiles', axis=1, tiled=True)]
    ppermute x0 -> x12, starting transfers between devices: none -> 15 us  [swap(): return lax.ppermute(x, 'tiles', [(i, i ^ bits) for i in range(peers)])]
    ppermute x0 -> x12, waiting for transfers between devices: none -> 13.9 us  [swap(): return lax.ppermute(x, 'tiles', [(i, i ^ bits) for i in range(peers)])]
    pallas_call x0 -> x8, Pallas kernels: none -> 13.3 us  [the longest x1 4.87 us: direct_and_emitted(): pl.pallas_call(functools.partial(direct_kernel, width), in_specs=[HBM, HB...]
    dot_general x3 -> x0, matrix products: 10.3 us -> none  [the longest x1 4.58 us: per_device(): direct = jnp.dot(sky, coeffs, preferred_element_type=jnp.float32)]
    reshape x1 -> x0, local copies, waits for them, and re-layouts: 5.98 us -> none  [per_device(): source_pool = everything.reshape(hour_count, peers * per_group, block_size)]
    gather x1 -> x0, local copies, waits for them, and re-layouts: 5.02 us -> none  [per_device(): sources = jnp.take(source_pool, block_cols, axis=1)]
    unnamed x6 -> x14, local copies, waits for them, and re-layouts: 0.01 us -> 1.12 us
  transfers between devices with their start and end apart: 1 -> 12, of which waited for: 1 -> 8; matrix products, arithmetic and copies ran while one was open for 0% -> 0% of each run, Pallas kernels for 0% -> 13%
where the time goes in v2:
time: 44.7 us; the launch traced here: 44.2 us
  starting transfers between devices  15 us (34%)
  waiting for transfers between devices  13.9 us (31%)
  Pallas kernels  13.3 us (30%)
  local copies, waits for them, and re-layouts  1.12 us (3%)
  between operations  0.79 us (2%)
    ppermute x12, starting transfers between devices, swap(): return lax.ppermute(x, 'tiles', [(i, i ^ bits) for i in range(peers)])  15 us
    ppermute x12, waiting for transfers between devices, swap(): return lax.ppermute(x, 'tiles', [(i, i ^ bits) for i in range(peers)])  13.9 us
    pallas_call x1, Pallas kernels, direct_and_emitted(): pl.pallas_call(functools.partial(direct_kernel, width), in_specs=[HBM, HB...  4.87 us
    pallas_call x3, Pallas kernels, reflect(): pl.pallas_call(functools.partial(reflect_kernel, phase), in_specs=[HBM, H...  4.87 us
    pallas_call x1, Pallas kernels, plan(): pl.pallas_call(functools.partial(plan_kernel, blocks, rooms, phase.shape[...  2.21 us
    pallas_call x2, Pallas kernels, pack(): pl.pallas_call(functools.partial(pack_kernel, wanted, groups), in_specs=[...  1.18 us
    unnamed x14, local copies, waits for them, and re-layouts  1.12 us
  transfers between devices with their start and end apart: 12, of which 8 were waited for; matrix products, arithmetic and copies ran while one was open for 0% of the time, Pallas kernels for 13%

profile of v2, /device:TPU:0, one launch (start us, length us, event | category | flops | bytes accessed | tf_op | source)
XLA Modules:
  0.0 44.2 jit_solution(11111508819735044728)
XLA Ops:
  0.0 0.0 copy-start.4
  0.0 0.0 copy-start.5
  0.0 0.0 copy-start.6
  0.0 0.0 copy-start
  0.0 0.0 copy-start.3
  0.0 0.0 copy-start.2
  0.0 4.9 %direct.1 = (f32[168,1024]{1,0:T(8,128)}, bf16[8,168,128]{2,1,0:T(8,128)(2,1)S(1)}) custom-call(bf16[168,2306]{1,0:T(8,128)(2,1)} %sky_ref.1, bf16[2306,1024]{1,0:T(8,128)(2,1)} %coeffs_ref.1, f32[1,1024]{1,0:T(1,128)} %bitcast.6), custom_call_target="tpu_custom_call" | custom-call | tf_op jit(solution)/shard_map/direct/pallas_call | solution.py:51
  4.9 3.0 %collective-permute-start.1 = (bf16[8,168,128]{2,1,0:T(8,128)(2,1)S(1)}, bf16[8,168,128]{2,1,0:T(8,128)(2,1)S(1)}, u32[]{:S(2)}, u32[]{:S(2)}) collective-permute-start(bf16[8,168,128]{2,1,0:T(8,128)(2,1)S(1)} %get-tuple-element.20.refs_0_), channel_id=1, source_target_pairs={{0,2},{1,3},{2,0},{3,1},{4,6},{5,7},{6,4},{7,5},{8,10},{9,11},{10,... | collective-permute-start | bytes 1032200 | tf_op jit(solution)/shard_map/ppermute | solution.py:220
  8.0 2.6 %collective-permute-start.6 = (bf16[8,168,128]{2,1,0:T(8,128)(2,1)S(1)}, bf16[8,168,128]{2,1,0:T(8,128)(2,1)S(1)}, u32[]{:S(2)}, u32[]{:S(2)}) collective-permute-start(bf16[8,168,128]{2,1,0:T(8,128)(2,1)S(1)} %get-tuple-element.20.refs_0_), channel_id=1, source_target_pairs={{0,8},{1,9},{2,10},{3,11},{4,12},{5,13},{6,14},{7,15},{8,0},{9,1},... | collective-permute-start | bytes 1032200 | tf_op jit(solution)/shard_map/ppermute | solution.py:220
  10.5 1.6 %collective-permute-start.5 = (bf16[8,168,128]{2,1,0:T(8,128)(2,1)S(1)}, bf16[8,168,128]{2,1,0:T(8,128)(2,1)S(1)}, u32[]{:S(2)}, u32[]{:S(2)}) collective-permute-start(bf16[8,168,128]{2,1,0:T(8,128)(2,1)S(1)} %get-tuple-element.20.refs_0_), channel_id=1, source_target_pairs={{0,4},{1,5},{2,6},{3,7},{4,0},{5,1},{6,2},{7,3},{8,12},{9,13},{10,... | collective-permute-start | bytes 1032200 | tf_op jit(solution)/shard_map/ppermute | solution.py:220
  12.8 0.0 copy-done.3
  12.8 0.2 reads.1.reads_ref
  13.0 0.1 collective-permute-start
  13.1 1.1 %collective-permute-done.table_ref = s32[1,128]{1,0:T(1,128)S(1)} collective-permute-done((s32[1,128]{1,0:T(1,128)S(1)}, s32[1,128]{1,0:T(1,128)S(1)}, u32[]{:S(2)}, u32[]{:S(2)}) %collective-permute-start) | collective-permute-done | bytes 544 | tf_op jit(solution)/shard_map/ppermute | solution.py:220
  14.2 1.9 %collective-permute-done.1.refs_1_.refs_3_ = bf16[8,168,128]{2,1,0:T(8,128)(2,1)S(1)} collective-permute-done((bf16[8,168,128]{2,1,0:T(8,128)(2,1)S(1)}, bf16[8,168,128]{2,1,0:T(8,128)(2,1)S(1)}, u32[]{:S(2)}, u32[]{:S(2)}) %collective-permute-start.1) | collective-permute-done | bytes 344096 | tf_op jit(solution)/shard_map/ppermute | solution.py:220
  16.0 0.6 %pack.2 = bf16[4,168,128]{2,1,0:T(8,128)(2,1)S(1)} custom-call(s32[1]{0:T(128)} %bitcast.me_ref, s32[1,128]{1,0:T(1,128)S(1)} %collective-permute-done.table_ref, bf16[8,168,128]{2,1,0:T(8,128)(2,1)S(1)} %get-tuple-element.20.refs_0_, bf16[8,168,128]{2,1,0:T(8,128)(2,1)S(1)} %collective-permute-done.1.refs_1_.refs_3_), custom_call_target="tpu_custom_call" | custom-call | tf_op jit(solution)/shard_map/pack/pallas_call | solution.py:104
  16.6 0.1 collective-permute-start.2
  16.7 1.8 %collective-permute-start.3 = (s32[1,128]{1,0:T(1,128)S(1)}, s32[1,128]{1,0:T(1,128)S(1)}, u32[]{:S(2)}, u32[]{:S(2)}) collective-permute-start(s32[1,128]{1,0:T(1,128)S(1)} %reads.1.reads_ref), channel_id=1, source_target_pairs={{0,2},{1,3},{2,0},{3,1},{4,6},{5,7},{6,4},{7,5},{8,10},{9,11},{10,... | collective-permute-start | bytes 1544 | tf_op jit(solution)/shard_map/ppermute | solution.py:220
  18.5 1.8 %collective-permute-done.3 = s32[1,128]{1,0:T(1,128)S(1)} collective-permute-done((s32[1,128]{1,0:T(1,128)S(1)}, s32[1,128]{1,0:T(1,128)S(1)}, u32[]{:S(2)}, u32[]{:S(2)}) %collective-permute-start.3) | collective-permute-done | bytes 544 | tf_op jit(solution)/shard_map/ppermute | solution.py:220
  20.3 1.8 %collective-permute-start.4 = (s32[2,128]{1,0:T(2,128)S(1)}, s32[2,128]{1,0:T(2,128)S(1)}, u32[]{:S(2)}, u32[]{:S(2)}) collective-permute-start(s32[2,128]{1,0:T(2,128)S(1)} %pad_add_fusion.1), channel_id=1, source_target_pairs={{0,4},{1,5},{2,6},{3,7},{4,0},{5,1},{6,2},{7,3},{8,12},{9,13},{10,... | collective-permute-start | bytes 3080 | tf_op jit(solution)/shard_map/ppermute | solution.py:220
  22.1 0.0 collective-permute-done.2.after_ref.refs_2_
  22.1 0.0 copy-done.4
  22.1 0.0 copy-done.5
  22.1 0.0 copy-done.6
  22.1 0.0 copy-done.2
  22.1 2.2 %plan.1.order_ref = s32[3,73]{1,0:T(4,128)S(1)} custom-call(s32[1]{0:T(128)} %bitcast.me_ref, s32[64]{0:T(128)S(1)} %copy-done.2, s32[64]{0:T(128)S(1)} %copy-done.3, s32[1,128]{1,0:T(1,128)S(1)} %reads.1.reads_ref, s32[16]{0:T(128)S(1)} %copy-done.6, s32[16]{0:T(128)S(1)} %copy-done.5, s32[16]{0:T(128)S(1)} %copy-done.4, ...), custom_call_target="tpu_custom_call" | custom-call | tf_op jit(solution)/shard_map/plan/pallas_call | solution.py:146
  24.3 1.8 %collective-permute-done.4 = s32[2,128]{1,0:T(2,128)S(1)} collective-permute-done((s32[2,128]{1,0:T(2,128)S(1)}, s32[2,128]{1,0:T(2,128)S(1)}, u32[]{:S(2)}, u32[]{:S(2)}) %collective-permute-start.4) | collective-permute-done | bytes 1056 | tf_op jit(solution)/shard_map/ppermute | solution.py:220
  26.1 0.0 collective-permute-done.6.refs_0_
  26.1 0.0 collective-permute-done.5.refs_2_
  26.1 0.0 collective-permute-start.8
  26.1 0.5 %collective-permute-start.7 = (bf16[8,168,128]{2,1,0:T(8,128)(2,1)S(1)}, bf16[8,168,128]{2,1,0:T(8,128)(2,1)S(1)}, u32[]{:S(2)}, u32[]{:S(2)}) collective-permute-start(bf16[8,168,128]{2,1,0:T(8,128)(2,1)S(1)} %collective-permute-done.6.refs_0_), channel_id=1, source_target_pairs={{0,1},{1,0},{2,3},{3,2},{4,5},{5,4},{6,7},{7,6},{8,9},{9,8},{10,11... | collective-permute-start | bytes 1032200 | tf_op jit(solution)/shard_map/ppermute | solution.py:220
  26.6 1.1 %collective-permute-done.8.refs_2_.refs_3_ = bf16[8,168,128]{2,1,0:T(8,128)(2,1)S(1)} collective-permute-done((bf16[8,168,128]{2,1,0:T(8,128)(2,1)S(1)}, bf16[8,168,128]{2,1,0:T(8,128)(2,1)S(1)}, u32[]{:S(2)}, u32[]{:S(2)}) %collective-permute-start.8) | collective-permute-done | bytes 344096 | tf_op jit(solution)/shard_map/ppermute | solution.py:220
  27.8 0.5 %collective-permute-done.7.refs_1_ = bf16[8,168,128]{2,1,0:T(8,128)(2,1)S(1)} collective-permute-done((bf16[8,168,128]{2,1,0:T(8,128)(2,1)S(1)}, bf16[8,168,128]{2,1,0:T(8,128)(2,1)S(1)}, u32[]{:S(2)}, u32[]{:S(2)}) %collective-permute-start.7) | collective-permute-done | bytes 344096 | tf_op jit(solution)/shard_map/ppermute | solution.py:220
  28.3 0.6 %pack.3 = (bf16[6,168,128]{2,1,0:T(8,128)(2,1)S(1)}, bf16[6,168,128]{2,1,0:T(8,128)(2,1)S(1)}, bf16[4,168,128]{2,1,0:T(8,128)(2,1)S(1)}) custom-call(s32[1]{0:T(128)} %bitcast.me_ref, s32[4,128]{1,0:T(4,128)S(1)} %pad_add_fusion.table_ref, bf16[8,168,128]{2,1,0:T(8,128)(2,1)S(1)} %collective-permute-done.6.refs_0_, ...), custom_call_target="tpu_custom_call" | custom-call | tf_op jit(solution)/shard_map/pack/pallas_call | solution.py:104
  28.9 0.5 %collective-permute-start.9 = (bf16[6,168,128]{2,1,0:T(8,128)(2,1)S(1)}, bf16[6,168,128]{2,1,0:T(8,128)(2,1)S(1)}, u32[]{:S(2)}, u32[]{:S(2)}) collective-permute-start(bf16[6,168,128]{2,1,0:T(8,128)(2,1)S(1)} %get-tuple-element.26), channel_id=1, source_target_pairs={{0,2},{1,3},{2,0},{3,1},{4,6},{5,7},{6,4},{7,5},{8,10},{9,11},{10,... | collective-permute-start | bytes 774152 | tf_op jit(solution)/shard_map/ppermute | solution.py:220
  29.4 1.5 %collective-permute-start.10 = (bf16[6,168,128]{2,1,0:T(8,128)(2,1)S(1)}, bf16[6,168,128]{2,1,0:T(8,128)(2,1)S(1)}, u32[]{:S(2)}, u32[]{:S(2)}) collective-permute-start(bf16[6,168,128]{2,1,0:T(8,128)(2,1)S(1)} %get-tuple-element.29), channel_id=1, source_target_pairs={{0,4},{1,5},{2,6},{3,7},{4,0},{5,1},{6,2},{7,3},{8,12},{9,13},{10,... | collective-permute-start | bytes 774152 | tf_op jit(solution)/shard_map/ppermute | solution.py:220
  30.9 1.5 %collective-permute-start.11 = (bf16[4,168,128]{2,1,0:T(8,128)(2,1)S(1)}, bf16[4,168,128]{2,1,0:T(8,128)(2,1)S(1)}, u32[]{:S(2)}, u32[]{:S(2)}) collective-permute-start(bf16[4,168,128]{2,1,0:T(8,128)(2,1)S(1)} %get-tuple-element.30), channel_id=1, source_target_pairs={{0,6},{1,7},{2,4},{3,5},{4,2},{5,3},{6,0},{7,1},{8,14},{9,15},{10,... | collective-permute-start | bytes 516104 | tf_op jit(solution)/shard_map/ppermute | solution.py:220
  32.4 0.0 copy-done
  32.4 0.0 copy-start.1
  32.4 1.1 %copy-done.1 = f32[168,1024]{1,0:T(8,128)S(1)} copy-done((f32[168,1024]{1,0:T(8,128)S(1)}, f32[168,1024]{1,0:T(8,128)}, u32[]{:S(2)}) %copy-start.1) | copy-done | bytes 688152
  33.5 1.2 %reflect.3.total_ref = f32[168,1024]{1,0:T(8,128)S(1)} custom-call(s32[3,73]{1,0:T(4,128)S(1)} %plan.1.order_ref, f32[168,1024]{1,0:T(8,128)S(1)} %copy-done.1, bf16[64,128,128]{2,1,0:T(8,128)(2,1)S(1)} %copy-done, bf16[8,168,128]{2,1,0:T(8,128)(2,1)S(1)} %get-tuple-element.20.refs_0_, bf16[8,168,128]{2,1,0:T(8,128)(2,1)S(1)} %collective-permute-done.1.refs_1_.refs_3_, ...), custom_call_target="tpu_custom_call" | custom-call | tf_op jit(solution)/shard_map/reflect/pallas_call | solution.py:195
  34.8 2.4 %collective-permute-done.9.refs_4_ = bf16[6,168,128]{2,1,0:T(8,128)(2,1)S(1)} collective-permute-done((bf16[6,168,128]{2,1,0:T(8,128)(2,1)S(1)}, bf16[6,168,128]{2,1,0:T(8,128)(2,1)S(1)}, u32[]{:S(2)}, u32[]{:S(2)}) %collective-permute-start.9) | collective-permute-done | bytes 258080 | tf_op jit(solution)/shard_map/ppermute | solution.py:220
  37.2 1.5 %reflect.4.total_ref = f32[168,1024]{1,0:T(8,128)S(1)} custom-call(s32[3,73]{1,0:T(4,128)S(1)} %plan.1.order_ref, f32[168,1024]{1,0:T(8,128)S(1)} %reflect.3.total_ref, bf16[64,128,128]{2,1,0:T(8,128)(2,1)S(1)} %copy-done, bf16[8,168,128]{2,1,0:T(8,128)(2,1)S(1)} %collective-permute-done.6.refs_0_, bf16[8,168,128]{2,1,0:T(8,128)(2,1)S(1)} %collective-permute-done.7.refs_1_, ...), custom_call_target="tpu_custom_call" | custom-call | tf_op jit(solution)/shard_map/reflect/pallas_call | solution.py:195
  38.8 3.3 %collective-permute-done.11.refs_1_ = bf16[4,168,128]{2,1,0:T(8,128)(2,1)S(1)} collective-permute-done((bf16[4,168,128]{2,1,0:T(8,128)(2,1)S(1)}, bf16[4,168,128]{2,1,0:T(8,128)(2,1)S(1)}, u32[]{:S(2)}, u32[]{:S(2)}) %collective-permute-start.11) | collective-permute-done | bytes 172064 | tf_op jit(solution)/shard_map/ppermute | solution.py:220
  42.1 0.0 collective-permute-done.10.refs_0_
  42.1 2.1 %reflect.5 = f32[168,1024]{1,0:T(8,128)} custom-call(s32[3,73]{1,0:T(4,128)S(1)} %plan.1.order_ref, f32[168,1024]{1,0:T(8,128)S(1)} %reflect.4.total_ref, bf16[64,128,128]{2,1,0:T(8,128)(2,1)S(1)} %copy-done, bf16[6,168,128]{2,1,0:T(8,128)(2,1)S(1)} %collective-permute-done.10.refs_0_, bf16[4,168,128]{2,1,0:T(8,128)(2,1)S(1)} %collective-permute-done.11.refs_1_), custom_call_target="tpu_custom_call" | custom-call | tf_op jit(solution)/shard_map/reflect/pallas_call | solution.py:195
  (3 shorter events, 0.0 us)
Async XLA Ops:
  0.0 22.1 %copy-start.4 = (s32[16]{0:T(128)S(1)}, s32[16]{0:T(128)}, u32[]{:S(2)}) copy-start(s32[16]{0:T(128)} %constant.14.clone.local_ref) | copy-start | bytes 196
  0.0 22.1 %copy-start.5 = (s32[16]{0:T(128)S(1)}, s32[16]{0:T(128)}, u32[]{:S(2)}) copy-start(s32[16]{0:T(128)} %constant.13.clone.base_ref) | copy-start | bytes 196
  0.0 22.1 %copy-start.6 = (s32[16]{0:T(128)S(1)}, s32[16]{0:T(128)}, u32[]{:S(2)}) copy-start(s32[16]{0:T(128)} %constant.12.clone.phase_ref) | copy-start | bytes 196
  0.0 32.4 %copy-start = (bf16[64,128,128]{2,1,0:T(8,128)(2,1)S(1)}, bf16[64,128,128]{2,1,0:T(8,128)(2,1)}, u32[]{:S(2)}) copy-start(bf16[64,128,128]{2,1,0:T(8,128)(2,1)} %views_ref.2) | copy-start | bytes 6291460
  0.0 12.8 %copy-start.3 = (s32[64]{0:T(128)S(1)}, s32[64]{0:T(128)}, u32[]{:S(2)}) copy-start(s32[64]{0:T(128)} %cols_ref.1) | copy-start | bytes 772
  0.0 22.1 %copy-start.2 = (s32[64]{0:T(128)S(1)}, s32[64]{0:T(128)}, u32[]{:S(2)}) copy-start(s32[64]{0:T(128)} %rows_ref.1) | copy-start | bytes 772
  4.9 11.1 %collective-permute-start.1 = (bf16[8,168,128]{2,1,0:T(8,128)(2,1)S(1)}, bf16[8,168,128]{2,1,0:T(8,128)(2,1)S(1)}, u32[]{:S(2)}, u32[]{:S(2)}) collective-permute-start(bf16[8,168,128]{2,1,0:T(8,128)(2,1)S(1)} %get-tuple-element.20.refs_0_), channel_id=1, source_target_pairs={{0,2},{1,3},{2,0},{3,1},{4,6},{5,7},{6,4},{7,5},{8,10},{9,11},{10,... | collective-permute-start | bytes 1032200 | tf_op jit(solution)/shard_map/ppermute | solution.py:220
  8.0 18.2 %collective-permute-start.6 = (bf16[8,168,128]{2,1,0:T(8,128)(2,1)S(1)}, bf16[8,168,128]{2,1,0:T(8,128)(2,1)S(1)}, u32[]{:S(2)}, u32[]{:S(2)}) collective-permute-start(bf16[8,168,128]{2,1,0:T(8,128)(2,1)S(1)} %get-tuple-element.20.refs_0_), channel_id=1, source_target_pairs={{0,8},{1,9},{2,10},{3,11},{4,12},{5,13},{6,14},{7,15},{8,0},{9,1},... | collective-permute-start | bytes 1032200 | tf_op jit(solution)/shard_map/ppermute | solution.py:220
  10.5 15.6 %collective-permute-start.5 = (bf16[8,168,128]{2,1,0:T(8,128)(2,1)S(1)}, bf16[8,168,128]{2,1,0:T(8,128)(2,1)S(1)}, u32[]{:S(2)}, u32[]{:S(2)}) collective-permute-start(bf16[8,168,128]{2,1,0:T(8,128)(2,1)S(1)} %get-tuple-element.20.refs_0_), channel_id=1, source_target_pairs={{0,4},{1,5},{2,6},{3,7},{4,0},{5,1},{6,2},{7,3},{8,12},{9,13},{10,... | collective-permute-start | bytes 1032200 | tf_op jit(solution)/shard_map/ppermute | solution.py:220
  13.0 1.2 %collective-permute-start = (s32[1,128]{1,0:T(1,128)S(1)}, s32[1,128]{1,0:T(1,128)S(1)}, u32[]{:S(2)}, u32[]{:S(2)}) collective-permute-start(s32[1,128]{1,0:T(1,128)S(1)} %reads.1.reads_ref), channel_id=1, source_target_pairs={{0,1},{1,0},{2,3},{3,2},{4,5},{5,4},{6,7},{7,6},{8,9},{9,8},{10,11... | collective-permute-start | bytes 1544 | tf_op jit(solution)/shard_map/ppermute | solution.py:220
  16.6 5.5 %collective-permute-start.2 = (bf16[4,168,128]{2,1,0:T(8,128)(2,1)S(1)}, bf16[4,168,128]{2,1,0:T(8,128)(2,1)S(1)}, u32[]{:S(2)}, u32[]{:S(2)}) collective-permute-start(bf16[4,168,128]{2,1,0:T(8,128)(2,1)S(1)} %pack.2), channel_id=1, source_target_pairs={{0,1},{1,0},{2,3},{3,2},{4,5},{5,4},{6,7},{7,6},{8,9},{9,8},{10,11... | collective-permute-start | bytes 516104 | tf_op jit(solution)/shard_map/ppermute | solution.py:220
  16.7 3.6 %collective-permute-start.3 = (s32[1,128]{1,0:T(1,128)S(1)}, s32[1,128]{1,0:T(1,128)S(1)}, u32[]{:S(2)}, u32[]{:S(2)}) collective-permute-start(s32[1,128]{1,0:T(1,128)S(1)} %reads.1.reads_ref), channel_id=1, source_target_pairs={{0,2},{1,3},{2,0},{3,1},{4,6},{5,7},{6,4},{7,5},{8,10},{9,11},{10,... | collective-permute-start | bytes 1544 | tf_op jit(solution)/shard_map/ppermute | solution.py:220
  20.3 5.8 %collective-permute-start.4 = (s32[2,128]{1,0:T(2,128)S(1)}, s32[2,128]{1,0:T(2,128)S(1)}, u32[]{:S(2)}, u32[]{:S(2)}) collective-permute-start(s32[2,128]{1,0:T(2,128)S(1)} %pad_add_fusion.1), channel_id=1, source_target_pairs={{0,4},{1,5},{2,6},{3,7},{4,0},{5,1},{6,2},{7,3},{8,12},{9,13},{10,... | collective-permute-start | bytes 3080 | tf_op jit(solution)/shard_map/ppermute | solution.py:220
  26.1 1.7 %collective-permute-start.8 = (bf16[8,168,128]{2,1,0:T(8,128)(2,1)S(1)}, bf16[8,168,128]{2,1,0:T(8,128)(2,1)S(1)}, u32[]{:S(2)}, u32[]{:S(2)}) collective-permute-start(bf16[8,168,128]{2,1,0:T(8,128)(2,1)S(1)} %collective-permute-done.5.refs_2_), channel_id=1, source_target_pairs={{0,1},{1,0},{2,3},{3,2},{4,5},{5,4},{6,7},{7,6},{8,9},{9,8},{10,11... | collective-permute-start | bytes 1032200 | tf_op jit(solution)/shard_map/ppermute | solution.py:220
  26.1 2.1 %collective-permute-start.7 = (bf16[8,168,128]{2,1,0:T(8,128)(2,1)S(1)}, bf16[8,168,128]{2,1,0:T(8,128)(2,1)S(1)}, u32[]{:S(2)}, u32[]{:S(2)}) collective-permute-start(bf16[8,168,128]{2,1,0:T(8,128)(2,1)S(1)} %collective-permute-done.6.refs_0_), channel_id=1, source_target_pairs={{0,1},{1,0},{2,3},{3,2},{4,5},{5,4},{6,7},{7,6},{8,9},{9,8},{10,11... | collective-permute-start | bytes 1032200 | tf_op jit(solution)/shard_map/ppermute | solution.py:220
  28.9 8.3 %collective-permute-start.9 = (bf16[6,168,128]{2,1,0:T(8,128)(2,1)S(1)}, bf16[6,168,128]{2,1,0:T(8,128)(2,1)S(1)}, u32[]{:S(2)}, u32[]{:S(2)}) collective-permute-start(bf16[6,168,128]{2,1,0:T(8,128)(2,1)S(1)} %get-tuple-element.26), channel_id=1, source_target_pairs={{0,2},{1,3},{2,0},{3,1},{4,6},{5,7},{6,4},{7,5},{8,10},{9,11},{10,... | collective-permute-start | bytes 774152 | tf_op jit(solution)/shard_map/ppermute | solution.py:220
  29.4 12.7 %collective-permute-start.10 = (bf16[6,168,128]{2,1,0:T(8,128)(2,1)S(1)}, bf16[6,168,128]{2,1,0:T(8,128)(2,1)S(1)}, u32[]{:S(2)}, u32[]{:S(2)}) collective-permute-start(bf16[6,168,128]{2,1,0:T(8,128)(2,1)S(1)} %get-tuple-element.29), channel_id=1, source_target_pairs={{0,4},{1,5},{2,6},{3,7},{4,0},{5,1},{6,2},{7,3},{8,12},{9,13},{10,... | collective-permute-start | bytes 774152 | tf_op jit(solution)/shard_map/ppermute | solution.py:220
  30.9 11.2 %collective-permute-start.11 = (bf16[4,168,128]{2,1,0:T(8,128)(2,1)S(1)}, bf16[4,168,128]{2,1,0:T(8,128)(2,1)S(1)}, u32[]{:S(2)}, u32[]{:S(2)}) collective-permute-start(bf16[4,168,128]{2,1,0:T(8,128)(2,1)S(1)} %get-tuple-element.30), channel_id=1, source_target_pairs={{0,6},{1,7},{2,4},{3,5},{4,2},{5,3},{6,0},{7,1},{8,14},{9,15},{10,... | collective-permute-start | bytes 516104 | tf_op jit(solution)/shard_map/ppermute | solution.py:220
  32.4 1.1 %copy-start.1 = (f32[168,1024]{1,0:T(8,128)S(1)}, f32[168,1024]{1,0:T(8,128)}, u32[]{:S(2)}) copy-start(f32[168,1024]{1,0:T(8,128)} %get-tuple-element.27.total_ref) | copy-start | bytes 2064388

commit v3 on v2

--- a/solution.py
+++ b/solution.py
@@ -15,56 +15,47 @@
 HBM = pl.BlockSpec(memory_space=pltpu.HBM)
 
 
-def direct_kernel(width, sky_ref, coeffs_ref, albedo_ref, direct_ref, emitted_ref, sky, coeffs, direct, sems):
-    blocks, _, block = emitted_ref.shape
+def product_kernel(width, after_ref, sky_ref, coeffs_ref, albedo_ref, out_ref, last_ref, sky, coeffs, sems):
+    del after_ref
     parts = coeffs.shape[0]
-    whole_sky = pltpu.make_async_copy(sky_ref, sky, sems.at[2 * parts])
+    whole_sky = pltpu.make_async_copy(sky_ref, sky, sems.at[parts])
     copies = [
         pltpu.make_async_copy(coeffs_ref.at[:, pl.ds(at * width, width)], coeffs.at[at], sems.at[at])
-        for at in range(parts)
-    ]
-    results = [
-        pltpu.make_async_copy(direct.at[at], direct_ref.at[:, pl.ds(at * width, width)], sems.at[parts + at])
         for at in range(parts)
     ]
     copies[0].start()
     whole_sky.start()
     for copy in copies[1:]:
         copy.start()
+    last_ref[...] = jnp.zeros_like(last_ref)
     whole_sky.wait()
     for at in range(parts):
         copies[at].wait()
-        part = jnp.dot(sky[...], coeffs[at], preferred_element_type=jnp.float32)
-        direct[at] = part
-        results[at].start()
-        emitted = (albedo_ref[:, at * width : (at + 1) * width] * part).astype(jnp.bfloat16)
+        direct = jnp.dot(sky[...], coeffs[at], preferred_element_type=jnp.float32)
+        if len(out_ref.shape) == 2:
+            out_ref[:, at * width : (at + 1) * width] = direct
+            continue
+        emitted = (albedo_ref[:, at * width : (at + 1) * width] * direct).astype(jnp.bfloat16)
+        block = out_ref.shape[2]
         for k in range(width // block):
-            emitted_ref[at * (width // block) + k] = emitted[:, k * block : (k + 1) * block]
-    for result in results:
-        result.wait()
-
-
-def direct_and_emitted(sky, coeffs, albedo, block, width):
-    hours, patches = sky.shape
-    tiles = coeffs.shape[1]
-    parts = tiles // width
-    return pl.pallas_call(
-        functools.partial(direct_kernel, width),
-        in_specs=[HBM, HBM, VMEM],
-        out_specs=[HBM, VMEM],
-        out_shape=[
-            jax.ShapeDtypeStruct((hours, tiles), jnp.float32),
-            pltpu.VMEM((tiles // block, hours, block), jnp.bfloat16),
-        ],
+            out_ref[at * (width // block) + k] = emitted[:, k * block : (k + 1) * block]
+
+
+def product(after, sky, coeffs, albedo, out, width, name):
+    parts = coeffs.shape[1] // width
+    return pl.pallas_call(
+        functools.partial(product_kernel, width),
+        in_specs=[ANY, HBM, HBM, VMEM],
+        out_specs=[VMEM, VMEM],
+        out_shape=[out, jax.ShapeDtypeStruct((1, 128), jnp.int32)],
         scratch_shapes=[
             pltpu.VMEM(sky.shape, sky.dtype),
-            pltpu.VMEM((parts, patches, width), coeffs.dtype),
-            pltpu.VMEM((parts, hours, width), jnp.float32),
-            pltpu.SemaphoreType.DMA((2 * parts + 1,)),
+            pltpu.VMEM((parts, coeffs.shape[0], width), coeffs.dtype),
+            pltpu.SemaphoreType.DMA((parts + 1,)),
         ],
-        compiler_params=pltpu.CompilerParams(vmem_limit_bytes=60 * 2**20),
-        name="direct",
-    )(sky, coeffs, albedo)
+        compiler_params=pltpu.CompilerParams(vmem_limit_bytes=62 * 2**20),
+        name=name,
+    )(after, sky, coeffs, albedo)
 
 
 def reads_kernel(blocks, groups, cols_ref, reads_ref):
@@ -111,8 +102,8 @@
     )(me, table, *held)
 
 
-def plan_kernel(blocks, rooms, groups, me_ref, rows_ref, cols_ref, reads_ref, phase_ref, base_ref, local_ref, after_ref, order_ref):
-    del after_ref
+def plan_kernel(blocks, rooms, groups, me_ref, rows_ref, cols_ref, reads_ref, phase_ref, base_ref, local_ref, *refs):
+    order_ref = refs[-1]
     phases, places = order_ref.shape
 
     def clear(i, carry):
@@ -145,12 +136,12 @@
 def plan(me, rows, cols, reads, phase, base, local, after, blocks, rooms):
     return pl.pallas_call(
         functools.partial(plan_kernel, blocks, rooms, phase.shape[0]),
-        in_specs=[SMEM] * 7 + [ANY],
+        in_specs=[SMEM] * 7 + [ANY] * len(after),
         out_specs=SMEM,
         out_shape=jax.ShapeDtypeStruct((len(rooms), 1 + rows.shape[0] + AT_ONCE), jnp.int32),
         compiler_params=pltpu.CompilerParams(vmem_limit_bytes=2**20),
         name="plan",
-    )(me, rows, cols, reads, phase, base, local, after)
+    )(me, rows, cols, reads, phase, base, local, *after)
 
 
 def reflect_kernel(phase, order_ref, total_ref, views_ref, *refs):
@@ -190,7 +181,7 @@
     lax.fori_loop(0, (order[phase, 0] + AT_ONCE - 1) // AT_ONCE, step, 0)
 
 
-def reflect(phase, order, total, views, sources):
+def reflect(phase, order, total, view_blocks, sources):
     room = sum(source.shape[0] for source in sources)
     return pl.pallas_call(
         functools.partial(reflect_kernel, phase),
@@ -204,7 +195,7 @@
         ],
         compiler_params=pltpu.CompilerParams(vmem_limit_bytes=24 * 2**20),
         name="reflect",
-    )(order, total, views, *sources)
+    )(order, total, view_blocks, *sources)
 
 
 def per_device(sky, coeffs, albedo, view_blocks, block_rows, block_cols, counts):
@@ -219,35 +210,30 @@
     def swap(x, bits):
         return lax.ppermute(x, "tiles", [(i, i ^ bits) for i in range(peers)])
 
-    direct, emitted = direct_and_emitted(sky, coeffs, albedo.reshape(1, -1), block, 4 * block)
-    counts, view_blocks, emitted = lax.optimization_barrier((counts, view_blocks, emitted))
+    hours, tiles = sky.shape[0], coeffs.shape[1]
+    albedo = albedo.reshape(1, -1)
+    emitted, zeros = product(
+        me, sky, coeffs, albedo, pltpu.VMEM((blocks, hours, block), jnp.bfloat16), 4 * block, "emitted"
+    )
 
     far_held = [swap(emitted, bits) for bits in far]
     below_held = swap(emitted, below)
     beside_held = swap(emitted, beside)
 
-    live = jnp.arange(block_cols.shape[0], dtype=jnp.int32) < counts[0]
+    live = jnp.arange(block_cols.shape[0], dtype=jnp.int32) < counts[0] + zeros[0, 0]
     reads = blocks_read(jnp.where(live, block_cols, -1), blocks, peers)
-    core_reads = swap(reads, core)
     table = jnp.concatenate([reads, swap(reads, beside)])
     below_table = swap(table, below)
-
-    (own,) = pack(
-        me, core_reads, peers, [emitted, beside_held], [(0, [(h, h * beside, end) for h in range(2) for end in range(2)])]
-    )
-    own = swap(own, core)
-
-    place = {
-        0: (0, 0),
-        beside: (0, blocks),
-        core: (0, 2 * blocks),
-        beside + core: (0, 2 * blocks + 2),
-        below: (1, 2 * blocks * rest),
-        below + core: (1, 2 * blocks * rest + blocks),
-        below + beside + core: (1, 2 * blocks * (rest + 1) + 4 * rest),
-        below + beside: (2, 4 * rest),
-    }
-    local = {0, beside, below, below + core}
+    direct, zeros = product(
+        reads, sky, coeffs, albedo, jax.ShapeDtypeStruct((hours, tiles), jnp.float32), 4 * block, "direct"
+    )
+
+    place = {kind: (0, blocks * kind) for kind in range(below)}
+    place[below] = (1, 2 * blocks * rest)
+    place[below + core] = (1, 2 * blocks * rest + blocks)
+    place[below + beside + core] = (1, 2 * blocks * (rest + 1) + 4 * rest)
+    place[below + beside] = (2, 4 * rest)
+    local = {*range(below), below, below + core}
     for h, bits in enumerate(far):
         for c in range(2):
             local.add(bits + c)
@@ -255,7 +241,7 @@
             place[bits + beside + c] = (1, 2 * blocks * (rest + 1) + 4 * h + 2 * c)
             place[bits + below + c] = (2, 4 * h + 2 * c)
             place[bits + below + beside + c] = (2, 4 * rest + 2 + 4 * h + 2 * c)
-    rooms = [2 * blocks + 4, 2 * blocks * (rest + 1) + 4 * rest + 2, 8 * rest + 2]
+    rooms = [4 * blocks, 2 * blocks * (rest + 1) + 4 * rest + 2, 8 * rest + 2]
     order = plan(
         me,
         block_rows,
@@ -264,7 +250,7 @@
         jnp.array([place[kind][0] for kind in range(peers)], jnp.int32),
         jnp.array([place[kind][1] for kind in range(peers)], jnp.int32),
         jnp.array([int(kind in local) for kind in range(peers)], jnp.int32),
-        own,
+        [zeros],
         blocks,
         rooms,
     )
@@ -272,6 +258,7 @@
     table = jnp.concatenate([table, below_table])
     held = [x for shard in far_held for x in (shard, swap(shard, core))]
     below_pair = [below_held, swap(below_held, core)]
+    near = [emitted, swap(emitted, core), beside_held, swap(beside_held, core)]
 
     wanted = [(2 * h + c, far[h] + c, end) for h in range(rest) for c in range(2) for end in range(2)]
     from_beside = [(2 * rest, below + core, end) for end in range(2)]
@@ -281,7 +268,7 @@
     late = [swap(x, bits) for x, bits in zip(others, (beside, below, below + beside))]
 
     direct, _ = lax.optimization_barrier((direct, others[0]))
-    total = reflect(0, order, direct, view_blocks, [emitted, beside_held, own])
+    total = reflect(0, order, direct, view_blocks, near)
     total = reflect(1, order, total, view_blocks, held + below_pair + late[:1])
     return reflect(2, order, total, view_blocks, late[1:])
 

time: 44.7 us -> 43.4 us (0.971)
  waiting for transfers between devices: 13.9 us -> 5.41 us
  Pallas kernels: 13.3 us -> 18.3 us
  local copies, waits for them, and re-layouts: 1.12 us -> 3.98 us
  starting transfers between devices: 15 us -> 12.9 us
  other arithmetic: 0.02 us -> 0.63 us
  between operations: 0.79 us -> 1.39 us
    ppermute x12, waiting for transfers between devices: 13.9 us -> 5.41 us  [swap(): return lax.ppermute(x, 'tiles', [(i, i ^ bits) for i in range(peers)])]
    pallas_call x1 -> x2, Pallas kernels: 4.87 us -> 8.87 us  [product(): pl.pallas_call(functools.partial(product_kernel, width), in_specs=[ANY, H...]
    unnamed x14 -> x22, local copies, waits for them, and re-layouts: 1.12 us -> 3.98 us
    ppermute x12, starting transfers between devices: 15 us -> 12.9 us  [swap(): return lax.ppermute(x, 'tiles', [(i, i ^ bits) for i in range(peers)])]
    pallas_call x3, Pallas kernels: 4.87 us -> 6.03 us  [reflect(): pl.pallas_call(functools.partial(reflect_kernel, phase), in_specs=[HBM, H...]
    concatenate x1, other arithmetic: 0.01 us -> 0.61 us  [per_device(): table = jnp.concatenate([table, below_table])]
    pallas_call x2 -> x1, Pallas kernels: 1.18 us -> 0.62 us  [pack(): pl.pallas_call(functools.partial(pack_kernel, wanted, groups), in_specs=[...]
  transfers between devices with their start and end apart: 12 -> 12, of which waited for: 8 -> 4; matrix products, arithmetic and copies ran while one was open for 0% -> 1% of each run, Pallas kernels for 13% -> 28%
where the time goes in v3:
time: 43.4 us; the launch traced here: 42.5 us
  Pallas kernels  18.3 us (42%)
  starting transfers between devices  12.9 us (30%)
  waiting for transfers between devices  5.41 us (12%)
  local copies, waits for them, and re-layouts  3.98 us (9%)
  between operations  1.39 us (3%)
  other arithmetic  0.63 us (1%)
    ppermute x12, starting transfers between devices, swap(): return lax.ppermute(x, 'tiles', [(i, i ^ bits) for i in range(peers)])  12.9 us
    pallas_call x2, Pallas kernels, product(): pl.pallas_call(functools.partial(product_kernel, width), in_specs=[ANY, H...  8.87 us
    pallas_call x3, Pallas kernels, reflect(): pl.pallas_call(functools.partial(reflect_kernel, phase), in_specs=[HBM, H...  6.03 us
    ppermute x12, waiting for transfers between devices, swap(): return lax.ppermute(x, 'tiles', [(i, i ^ bits) for i in range(peers)])  5.41 us
    unnamed x22, local copies, waits for them, and re-layouts  3.98 us
    pallas_call x1, Pallas kernels, plan(): pl.pallas_call(functools.partial(plan_kernel, blocks, rooms, phase.shape[...  2.57 us
  transfers between devices with their start and end apart: 12, of which 4 were waited for; matrix products, arithmetic and copies ran while one was open for 1% of the time, Pallas kernels for 28%

profile of v3, /device:TPU:0, one launch (start us, length us, event | category | flops | bytes accessed | tf_op | source)
XLA Modules:
  0.0 42.5 jit_solution(8167147634157293147)
XLA Ops:
  0.0 0.0 copy-start.6
  0.0 0.0 copy-start.5
  0.0 0.0 copy-start.7
  0.0 0.0 copy-start.8
  0.0 0.0 copy-start.9
  0.0 4.0 %emitted.1 = (bf16[8,168,128]{2,1,0:T(8,128)(2,1)S(1)}, s32[1,128]{1,0:T(1,128)}) custom-call(s32[1]{0:T(128)} %bitcast.after_ref.me_ref, bf16[168,2306]{1,0:T(8,128)(2,1)} %sky_ref.3, bf16[2306,1024]{1,0:T(8,128)(2,1)} %coeffs_ref.3, f32[1,1024]{1,0:T(1,128)} %bitcast.8), custom_call_target="tpu_custom_call" | custom-call | tf_op jit(solution)/shard_map/emitted/pallas_call | solution.py:46
  4.1 4.1 %collective-permute-start.3 = (bf16[8,168,128]{2,1,0:T(8,128)(2,1)S(1)}, bf16[8,168,128]{2,1,0:T(8,128)(2,1)S(1)}, u32[]{:S(2)}, u32[]{:S(2)}) collective-permute-start(bf16[8,168,128]{2,1,0:T(8,128)(2,1)S(1)} %get-tuple-element.19.refs_0_), channel_id=1, source_target_pairs={{0,8},{1,9},{2,10},{3,11},{4,12},{5,13},{6,14},{7,15},{8,0},{9,1},... | collective-permute-start | bytes 1032200 | tf_op jit(solution)/shard_map/ppermute | solution.py:211
  8.2 1.6 %collective-permute-start.2 = (bf16[8,168,128]{2,1,0:T(8,128)(2,1)S(1)}, bf16[8,168,128]{2,1,0:T(8,128)(2,1)S(1)}, u32[]{:S(2)}, u32[]{:S(2)}) collective-permute-start(bf16[8,168,128]{2,1,0:T(8,128)(2,1)S(1)} %get-tuple-element.19.refs_0_), channel_id=1, source_target_pairs={{0,4},{1,5},{2,6},{3,7},{4,0},{5,1},{6,2},{7,3},{8,12},{9,13},{10,... | collective-permute-start | bytes 1032200 | tf_op jit(solution)/shard_map/ppermute | solution.py:211
  11.0 0.0 copy-done.6
  11.0 0.2 reads.1.after_ref.reads_ref
  11.2 0.0 copy-start.3
  11.2 1.6 %collective-permute-start = (s32[1,128]{1,0:T(1,128)S(1)}, s32[1,128]{1,0:T(1,128)S(1)}, u32[]{:S(2)}, u32[]{:S(2)}) collective-permute-start(s32[1,128]{1,0:T(1,128)S(1)} %reads.1.after_ref.reads_ref), channel_id=1, source_target_pairs={{0,2},{1,3},{2,0},{3,1},{4,6},{5,7},{6,4},{7,5},{8,10},{9,11},{10,... | collective-permute-start | bytes 1544 | tf_op jit(solution)/shard_map/ppermute | solution.py:211
  12.8 0.5 %collective-permute-start.6 = (bf16[8,168,128]{2,1,0:T(8,128)(2,1)S(1)}, bf16[8,168,128]{2,1,0:T(8,128)(2,1)S(1)}, u32[]{:S(2)}, u32[]{:S(2)}) collective-permute-start(bf16[8,168,128]{2,1,0:T(8,128)(2,1)S(1)} %get-tuple-element.19.refs_0_), channel_id=1, source_target_pairs={{0,2},{1,3},{2,0},{3,1},{4,6},{5,7},{6,4},{7,5},{8,10},{9,11},{10,... | collective-permute-start | bytes 1032200 | tf_op jit(solution)/shard_map/ppermute | solution.py:211
  13.3 1.5 %collective-permute-done = s32[1,128]{1,0:T(1,128)S(1)} collective-permute-done((s32[1,128]{1,0:T(1,128)S(1)}, s32[1,128]{1,0:T(1,128)S(1)}, u32[]{:S(2)}, u32[]{:S(2)}) %collective-permute-start) | collective-permute-done | bytes 544 | tf_op jit(solution)/shard_map/ppermute | solution.py:211
  14.8 0.4 %collective-permute-start.1 = (s32[2,128]{1,0:T(2,128)S(1)}, s32[2,128]{1,0:T(2,128)S(1)}, u32[]{:S(2)}, u32[]{:S(2)}) collective-permute-start(s32[2,128]{1,0:T(2,128)S(1)} %pad_add_fusion.1), channel_id=1, source_target_pairs={{0,4},{1,5},{2,6},{3,7},{4,0},{5,1},{6,2},{7,3},{8,12},{9,13},{10,... | collective-permute-start | bytes 3080 | tf_op jit(solution)/shard_map/ppermute | solution.py:211
  15.3 0.0 copy-done.3
  15.3 4.8 %direct.1 = (f32[168,1024]{1,0:T(8,128)}, s32[1,128]{1,0:T(1,128)}) custom-call(s32[1,128]{1,0:T(1,128)} %copy-done.3, bf16[168,2306]{1,0:T(8,128)(2,1)} %sky_ref.3, bf16[2306,1024]{1,0:T(8,128)(2,1)} %coeffs_ref.3, f32[1,1024]{1,0:T(1,128)} %bitcast.9), custom_call_target="tpu_custom_call" | custom-call | tf_op jit(solution)/shard_map/direct/pallas_call | solution.py:46
  20.1 0.0 copy-done.5
  20.1 0.0 copy-done.7
  20.1 0.0 copy-done.8
  20.1 0.0 copy-done.9
  20.1 0.0 copy-start.4
  20.1 0.6 %copy-done.4 = s32[1,128]{1,0:T(1,128)S(1)} copy-done((s32[1,128]{1,0:T(1,128)S(1)}, s32[1,128]{1,0:T(1,128)}, u32[]{:S(2)}) %copy-start.4) | copy-done | bytes 536
  20.7 0.0 copy-start.10
  20.7 0.7 %copy-done.10 = s32[1,128]{1,0:T(1,128)S(1)} copy-done((s32[1,128]{1,0:T(1,128)S(1)}, s32[1,128]{1,0:T(1,128)}, u32[]{:S(2)}) %copy-start.10) | copy-done | bytes 536
  21.4 2.6 %plan.1.order_ref = s32[3,73]{1,0:T(4,128)S(1)} custom-call(s32[1]{0:T(128)} %bitcast.after_ref.me_ref, s32[64]{0:T(128)S(1)} %copy-done.5, s32[64]{0:T(128)S(1)} %copy-done.6, s32[1,128]{1,0:T(1,128)S(1)} %copy-done.4, s32[16]{0:T(128)S(1)} %copy-done.9, s32[16]{0:T(128)S(1)} %copy-done.8, s32[16]{0:T(128)S(1)} %copy-done.7, s32[1,128]{1,0:T(1,128)S(1)} %copy-done.10), custom_call_target="tpu_custom_call" | custom-call | tf_op jit(solution)/shard_map/plan/pallas_call | solution.py:137
  24.0 0.0 collective-permute-done.1
  24.0 0.0 collective-permute-done.3.refs_0_
  24.0 0.0 collective-permute-done.2.refs_2_
  24.0 0.1 collective-permute-start.5
  24.1 0.5 %collective-permute-start.4 = (bf16[8,168,128]{2,1,0:T(8,128)(2,1)S(1)}, bf16[8,168,128]{2,1,0:T(8,128)(2,1)S(1)}, u32[]{:S(2)}, u32[]{:S(2)}) collective-permute-start(bf16[8,168,128]{2,1,0:T(8,128)(2,1)S(1)} %collective-permute-done.3.refs_0_), channel_id=1, source_target_pairs={{0,1},{1,0},{2,3},{3,2},{4,5},{5,4},{6,7},{7,6},{8,9},{9,8},{10,11... | collective-permute-start | bytes 1032200 | tf_op jit(solution)/shard_map/ppermute | solution.py:211
  24.6 0.1 collective-permute-start.7
  24.7 0.0 collective-permute-done.6.refs_3_.refs_2_
  24.7 0.4 %collective-permute-start.8 = (bf16[8,168,128]{2,1,0:T(8,128)(2,1)S(1)}, bf16[8,168,128]{2,1,0:T(8,128)(2,1)S(1)}, u32[]{:S(2)}, u32[]{:S(2)}) collective-permute-start(bf16[8,168,128]{2,1,0:T(8,128)(2,1)S(1)} %collective-permute-done.6.refs_3_.refs_2_), channel_id=1, source_target_pairs={{0,1},{1,0},{2,3},{3,2},{4,5},{5,4},{6,7},{7,6},{8,9},{9,8},{10,11... | collective-permute-start | bytes 1032200 | tf_op jit(solution)/shard_map/ppermute | solution.py:211
  25.1 0.6 %pad_add_fusion.table_ref = s32[4,128]{1,0:T(4,128)S(1)} fusion(s32[2,128]{1,0:T(2,128)S(1)} %collective-permute-done.1, s32[1,128]{1,0:T(1,128)S(1)} %collective-permute-done, s32[1,128]{1,0:T(1,128)} %copy-done.3), kind=kLoop, calls=%fused_computation | loop fusion | flops 1024 | bytes 4096 | tf_op jit(solution)/shard_map/concatenate | solution.py:258
  25.7 0.0 collective-permute-done.5.refs_2_.refs_3_
  25.7 0.5 %collective-permute-done.4.refs_1_ = bf16[8,168,128]{2,1,0:T(8,128)(2,1)S(1)} collective-permute-done((bf16[8,168,128]{2,1,0:T(8,128)(2,1)S(1)}, bf16[8,168,128]{2,1,0:T(8,128)(2,1)S(1)}, u32[]{:S(2)}, u32[]{:S(2)}) %collective-permute-start.4) | collective-permute-done | bytes 344096 | tf_op jit(solution)/shard_map/ppermute | solution.py:211
  26.2 0.6 %pack.1 = (bf16[6,168,128]{2,1,0:T(8,128)(2,1)S(1)}, bf16[6,168,128]{2,1,0:T(8,128)(2,1)S(1)}, bf16[4,168,128]{2,1,0:T(8,128)(2,1)S(1)}) custom-call(s32[1]{0:T(128)} %bitcast.after_ref.me_ref, s32[4,128]{1,0:T(4,128)S(1)} %pad_add_fusion.table_ref, bf16[8,168,128]{2,1,0:T(8,128)(2,1)S(1)} %collective-permute-done.3.refs_0_, ...), custom_call_target="tpu_custom_call" | custom-call | tf_op jit(solution)/shard_map/pack/pallas_call | solution.py:95
  26.8 1.6 %collective-permute-start.9 = (bf16[6,168,128]{2,1,0:T(8,128)(2,1)S(1)}, bf16[6,168,128]{2,1,0:T(8,128)(2,1)S(1)}, u32[]{:S(2)}, u32[]{:S(2)}) collective-permute-start(bf16[6,168,128]{2,1,0:T(8,128)(2,1)S(1)} %get-tuple-element.25), channel_id=1, source_target_pairs={{0,2},{1,3},{2,0},{3,1},{4,6},{5,7},{6,4},{7,5},{8,10},{9,11},{10,... | collective-permute-start | bytes 774152 | tf_op jit(solution)/shard_map/ppermute | solution.py:211
  28.5 1.6 %collective-permute-start.10 = (bf16[6,168,128]{2,1,0:T(8,128)(2,1)S(1)}, bf16[6,168,128]{2,1,0:T(8,128)(2,1)S(1)}, u32[]{:S(2)}, u32[]{:S(2)}) collective-permute-start(bf16[6,168,128]{2,1,0:T(8,128)(2,1)S(1)} %get-tuple-element.27), channel_id=1, source_target_pairs={{0,4},{1,5},{2,6},{3,7},{4,0},{5,1},{6,2},{7,3},{8,12},{9,13},{10,... | collective-permute-start | bytes 774152 | tf_op jit(solution)/shard_map/ppermute | solution.py:211
  30.1 0.3 collective-permute-start.11
  30.4 0.0 collective-permute-done.7.refs_1_
  30.4 0.0 collective-permute-done.8.refs_3_
  30.4 0.0 copy-start
  30.4 1.6 %copy-done = bf16[64,128,128]{2,1,0:T(8,128)(2,1)S(1)} copy-done((bf16[64,128,128]{2,1,0:T(8,128)(2,1)S(1)}, bf16[64,128,128]{2,1,0:T(8,128)(2,1)}, u32[]{:S(2)}) %copy-start) | copy-done | bytes 2097176
  32.0 0.0 copy-start.2
  32.0 1.1 %copy-done.2 = f32[168,1024]{1,0:T(8,128)S(1)} copy-done((f32[168,1024]{1,0:T(8,128)S(1)}, f32[168,1024]{1,0:T(8,128)}, u32[]{:S(2)}) %copy-start.2) | copy-done | bytes 688152
  33.1 0.0 copy-start.1
  33.1 1.6 %reflect.3.total_ref = f32[168,1024]{1,0:T(8,128)S(1)} custom-call(s32[3,73]{1,0:T(4,128)S(1)} %plan.1.order_ref, f32[168,1024]{1,0:T(8,128)S(1)} %copy-done.2, bf16[64,128,128]{2,1,0:T(8,128)(2,1)S(1)} %copy-done, bf16[8,168,128]{2,1,0:T(8,128)(2,1)S(1)} %get-tuple-element.19.refs_0_, bf16[8,168,128]{2,1,0:T(8,128)(2,1)S(1)} %collective-permute-done.7.refs_1_, ...), custom_call_target="tpu_custom_call" | custom-call | tf_op jit(solution)/shard_map/reflect/pallas_call | solution.py:186
  34.7 0.4 %collective-permute-done.9.refs_4_ = bf16[6,168,128]{2,1,0:T(8,128)(2,1)S(1)} collective-permute-done((bf16[6,168,128]{2,1,0:T(8,128)(2,1)S(1)}, bf16[6,168,128]{2,1,0:T(8,128)(2,1)S(1)}, u32[]{:S(2)}, u32[]{:S(2)}) %collective-permute-start.9) | collective-permute-done | bytes 258080 | tf_op jit(solution)/shard_map/ppermute | solution.py:211
  35.2 0.0 copy-done.1
  35.2 1.9 %reflect.4.total_ref = f32[168,1024]{1,0:T(8,128)S(1)} custom-call(s32[3,73]{1,0:T(4,128)S(1)} %plan.1.order_ref, f32[168,1024]{1,0:T(8,128)S(1)} %reflect.3.total_ref, bf16[64,128,128]{2,1,0:T(8,128)(2,1)S(1)} %copy-done.1, bf16[8,168,128]{2,1,0:T(8,128)(2,1)S(1)} %collective-permute-done.3.refs_0_, ...), custom_call_target="tpu_custom_call" | custom-call | tf_op jit(solution)/shard_map/reflect/pallas_call | solution.py:186
  37.1 2.9 %collective-permute-done.11.refs_1_ = bf16[4,168,128]{2,1,0:T(8,128)(2,1)S(1)} collective-permute-done((bf16[4,168,128]{2,1,0:T(8,128)(2,1)S(1)}, bf16[4,168,128]{2,1,0:T(8,128)(2,1)S(1)}, u32[]{:S(2)}, u32[]{:S(2)}) %collective-permute-start.11) | collective-permute-done | bytes 172064 | tf_op jit(solution)/shard_map/ppermute | solution.py:211
  40.0 0.0 collective-permute-done.10.refs_0_
  40.0 2.5 %reflect.5 = f32[168,1024]{1,0:T(8,128)} custom-call(s32[3,73]{1,0:T(4,128)S(1)} %plan.1.order_ref, f32[168,1024]{1,0:T(8,128)S(1)} %reflect.4.total_ref, bf16[64,128,128]{2,1,0:T(8,128)(2,1)S(1)} %copy-done.1, bf16[6,168,128]{2,1,0:T(8,128)(2,1)S(1)} %collective-permute-done.10.refs_0_, bf16[4,168,128]{2,1,0:T(8,128)(2,1)S(1)} %collective-permute-done.11.refs_1_), custom_call_target="tpu_custom_call" | custom-call | tf_op jit(solution)/shard_map/reflect/pallas_call | solution.py:186
  (2 shorter events, 0.0 us)
Async XLA Ops:
  0.0 11.0 %copy-start.6 = (s32[64]{0:T(128)S(1)}, s32[64]{0:T(128)}, u32[]{:S(2)}) copy-start(s32[64]{0:T(128)} %cols_ref.1) | copy-start | bytes 772
  0.0 20.1 %copy-start.5 = (s32[64]{0:T(128)S(1)}, s32[64]{0:T(128)}, u32[]{:S(2)}) copy-start(s32[64]{0:T(128)} %rows_ref.1) | copy-start | bytes 772
  0.0 20.1 %copy-start.7 = (s32[16]{0:T(128)S(1)}, s32[16]{0:T(128)}, u32[]{:S(2)}) copy-start(s32[16]{0:T(128)} %constant.14.clone.local_ref) | copy-start | bytes 196
  0.0 20.1 %copy-start.8 = (s32[16]{0:T(128)S(1)}, s32[16]{0:T(128)}, u32[]{:S(2)}) copy-start(s32[16]{0:T(128)} %constant.13.clone.base_ref) | copy-start | bytes 196
  0.0 20.1 %copy-start.9 = (s32[16]{0:T(128)S(1)}, s32[16]{0:T(128)}, u32[]{:S(2)}) copy-start(s32[16]{0:T(128)} %constant.12.clone.phase_ref) | copy-start | bytes 196
  4.1 19.9 %collective-permute-start.3 = (bf16[8,168,128]{2,1,0:T(8,128)(2,1)S(1)}, bf16[8,168,128]{2,1,0:T(8,128)(2,1)S(1)}, u32[]{:S(2)}, u32[]{:S(2)}) collective-permute-start(bf16[8,168,128]{2,1,0:T(8,128)(2,1)S(1)} %get-tuple-element.19.refs_0_), channel_id=1, source_target_pairs={{0,8},{1,9},{2,10},{3,11},{4,12},{5,13},{6,14},{7,15},{8,0},{9,1},... | collective-permute-start | bytes 1032200 | tf_op jit(solution)/shard_map/ppermute | solution.py:211
  8.2 15.8 %collective-permute-start.2 = (bf16[8,168,128]{2,1,0:T(8,128)(2,1)S(1)}, bf16[8,168,128]{2,1,0:T(8,128)(2,1)S(1)}, u32[]{:S(2)}, u32[]{:S(2)}) collective-permute-start(bf16[8,168,128]{2,1,0:T(8,128)(2,1)S(1)} %get-tuple-element.19.refs_0_), channel_id=1, source_target_pairs={{0,4},{1,5},{2,6},{3,7},{4,0},{5,1},{6,2},{7,3},{8,12},{9,13},{10,... | collective-permute-start | bytes 1032200 | tf_op jit(solution)/shard_map/ppermute | solution.py:211
  11.2 4.1 %copy-start.3 = (s32[1,128]{1,0:T(1,128)}, s32[1,128]{1,0:T(1,128)S(1)}, u32[]{:S(2)}) copy-start(s32[1,128]{1,0:T(1,128)S(1)} %reads.1.after_ref.reads_ref) | copy-start | bytes 1540
  11.2 3.6 %collective-permute-start = (s32[1,128]{1,0:T(1,128)S(1)}, s32[1,128]{1,0:T(1,128)S(1)}, u32[]{:S(2)}, u32[]{:S(2)}) collective-permute-start(s32[1,128]{1,0:T(1,128)S(1)} %reads.1.after_ref.reads_ref), channel_id=1, source_target_pairs={{0,2},{1,3},{2,0},{3,1},{4,6},{5,7},{6,4},{7,5},{8,10},{9,11},{10,... | collective-permute-start | bytes 1544 | tf_op jit(solution)/shard_map/ppermute | solution.py:211
  12.8 11.9 %collective-permute-start.6 = (bf16[8,168,128]{2,1,0:T(8,128)(2,1)S(1)}, bf16[8,168,128]{2,1,0:T(8,128)(2,1)S(1)}, u32[]{:S(2)}, u32[]{:S(2)}) collective-permute-start(bf16[8,168,128]{2,1,0:T(8,128)(2,1)S(1)} %get-tuple-element.19.refs_0_), channel_id=1, source_target_pairs={{0,2},{1,3},{2,0},{3,1},{4,6},{5,7},{6,4},{7,5},{8,10},{9,11},{10,... | collective-permute-start | bytes 1032200 | tf_op jit(solution)/shard_map/ppermute | solution.py:211
  14.8 9.2 %collective-permute-start.1 = (s32[2,128]{1,0:T(2,128)S(1)}, s32[2,128]{1,0:T(2,128)S(1)}, u32[]{:S(2)}, u32[]{:S(2)}) collective-permute-start(s32[2,128]{1,0:T(2,128)S(1)} %pad_add_fusion.1), channel_id=1, source_target_pairs={{0,4},{1,5},{2,6},{3,7},{4,0},{5,1},{6,2},{7,3},{8,12},{9,13},{10,... | collective-permute-start | bytes 3080 | tf_op jit(solution)/shard_map/ppermute | solution.py:211
  20.1 0.6 %copy-start.4 = (s32[1,128]{1,0:T(1,128)S(1)}, s32[1,128]{1,0:T(1,128)}, u32[]{:S(2)}) copy-start(s32[1,128]{1,0:T(1,128)} %copy-done.3) | copy-start | bytes 1540
  20.7 0.7 %copy-start.10 = (s32[1,128]{1,0:T(1,128)S(1)}, s32[1,128]{1,0:T(1,128)}, u32[]{:S(2)}) copy-start(s32[1,128]{1,0:T(1,128)} %get-tuple-element.18.refs_0_) | copy-start | bytes 1540
  24.0 1.7 %collective-permute-start.5 = (bf16[8,168,128]{2,1,0:T(8,128)(2,1)S(1)}, bf16[8,168,128]{2,1,0:T(8,128)(2,1)S(1)}, u32[]{:S(2)}, u32[]{:S(2)}) collective-permute-start(bf16[8,168,128]{2,1,0:T(8,128)(2,1)S(1)} %collective-permute-done.2.refs_2_), channel_id=1, source_target_pairs={{0,1},{1,0},{2,3},{3,2},{4,5},{5,4},{6,7},{7,6},{8,9},{9,8},{10,11... | collective-permute-start | bytes 1032200 | tf_op jit(solution)/shard_map/ppermute | solution.py:211
  24.1 2.1 %collective-permute-start.4 = (bf16[8,168,128]{2,1,0:T(8,128)(2,1)S(1)}, bf16[8,168,128]{2,1,0:T(8,128)(2,1)S(1)}, u32[]{:S(2)}, u32[]{:S(2)}) collective-permute-start(bf16[8,168,128]{2,1,0:T(8,128)(2,1)S(1)} %collective-permute-done.3.refs_0_), channel_id=1, source_target_pairs={{0,1},{1,0},{2,3},{3,2},{4,5},{5,4},{6,7},{7,6},{8,9},{9,8},{10,11... | collective-permute-start | bytes 1032200 | tf_op jit(solution)/shard_map/ppermute | solution.py:211
  24.6 5.8 %collective-permute-start.7 = (bf16[8,168,128]{2,1,0:T(8,128)(2,1)S(1)}, bf16[8,168,128]{2,1,0:T(8,128)(2,1)S(1)}, u32[]{:S(2)}, u32[]{:S(2)}) collective-permute-start(bf16[8,168,128]{2,1,0:T(8,128)(2,1)S(1)} %get-tuple-element.19.refs_0_), channel_id=1, source_target_pairs={{0,1},{1,0},{2,3},{3,2},{4,5},{5,4},{6,7},{7,6},{8,9},{9,8},{10,11... | collective-permute-start | bytes 1032200 | tf_op jit(solution)/shard_map/ppermute | solution.py:211
  24.7 5.7 %collective-permute-start.8 = (bf16[8,168,128]{2,1,0:T(8,128)(2,1)S(1)}, bf16[8,168,128]{2,1,0:T(8,128)(2,1)S(1)}, u32[]{:S(2)}, u32[]{:S(2)}) collective-permute-start(bf16[8,168,128]{2,1,0:T(8,128)(2,1)S(1)} %collective-permute-done.6.refs_3_.refs_2_), channel_id=1, source_target_pairs={{0,1},{1,0},{2,3},{3,2},{4,5},{5,4},{6,7},{7,6},{8,9},{9,8},{10,11... | collective-permute-start | bytes 1032200 | tf_op jit(solution)/shard_map/ppermute | solution.py:211
  26.8 8.3 %collective-permute-start.9 = (bf16[6,168,128]{2,1,0:T(8,128)(2,1)S(1)}, bf16[6,168,128]{2,1,0:T(8,128)(2,1)S(1)}, u32[]{:S(2)}, u32[]{:S(2)}) collective-permute-start(bf16[6,168,128]{2,1,0:T(8,128)(2,1)S(1)} %get-tuple-element.25), channel_id=1, source_target_pairs={{0,2},{1,3},{2,0},{3,1},{4,6},{5,7},{6,4},{7,5},{8,10},{9,11},{10,... | collective-permute-start | bytes 774152 | tf_op jit(solution)/shard_map/ppermute | solution.py:211
  28.5 11.5 %collective-permute-start.10 = (bf16[6,168,128]{2,1,0:T(8,128)(2,1)S(1)}, bf16[6,168,128]{2,1,0:T(8,128)(2,1)S(1)}, u32[]{:S(2)}, u32[]{:S(2)}) collective-permute-start(bf16[6,168,128]{2,1,0:T(8,128)(2,1)S(1)} %get-tuple-element.27), channel_id=1, source_target_pairs={{0,4},{1,5},{2,6},{3,7},{4,0},{5,1},{6,2},{7,3},{8,12},{9,13},{10,... | collective-permute-start | bytes 774152 | tf_op jit(solution)/shard_map/ppermute | solution.py:211
  30.1 10.0 %collective-permute-start.11 = (bf16[4,168,128]{2,1,0:T(8,128)(2,1)S(1)}, bf16[4,168,128]{2,1,0:T(8,128)(2,1)S(1)}, u32[]{:S(2)}, u32[]{:S(2)}) collective-permute-start(bf16[4,168,128]{2,1,0:T(8,128)(2,1)S(1)} %get-tuple-element.28), channel_id=1, source_target_pairs={{0,6},{1,7},{2,4},{3,5},{4,2},{5,3},{6,0},{7,1},{8,14},{9,15},{10,... | collective-permute-start | bytes 516104 | tf_op jit(solution)/shard_map/ppermute | solution.py:211
  30.4 1.6 %copy-start = (bf16[64,128,128]{2,1,0:T(8,128)(2,1)S(1)}, bf16[64,128,128]{2,1,0:T(8,128)(2,1)}, u32[]{:S(2)}) copy-start(bf16[64,128,128]{2,1,0:T(8,128)(2,1)} %views_ref.5) | copy-start | bytes 6291460
  32.0 1.1 %copy-start.2 = (f32[168,1024]{1,0:T(8,128)S(1)}, f32[168,1024]{1,0:T(8,128)}, u32[]{:S(2)}) copy-start(f32[168,1024]{1,0:T(8,128)} %get-tuple-element.26.total_ref) | copy-start | bytes 2064388
  33.1 2.1 %copy-start.1 = (bf16[64,128,128]{2,1,0:T(8,128)(2,1)S(1)}, bf16[64,128,128]{2,1,0:T(8,128)(2,1)}, u32[]{:S(2)}) copy-start(bf16[64,128,128]{2,1,0:T(8,128)(2,1)} %views_ref.5) | copy-start | bytes 6291460
